TPU v7x, 32 devices: a whole 2x2x4 slice. The times are simulated.
32 devices in a mesh: dp: 2 (over core), blk: 16 (over z, y, x).
Axes of the slice: x: 2, y: 2, z: 4, core: 2. Of those that a mesh axis runs over, the one named last changes fastest.
Arguments:
- inputs: bfloat16 [4, 1024, 1024], P('dp', 'blk'), may hold values from -6 to 6
- segments: int32 [4, 1024], P('dp', 'blk'), may hold values from 0 to 7, as said below
- pad_mask: int32 [4, 1024], P('dp', 'blk'), may hold values from 0 to 1, as said below
- timesteps: int32 [4, 8], P('dp'), may hold values from 0 to 4999
- w_qkv: bfloat16 [1024, 3072], P(('dp', 'blk')), may hold values from -0.1875 to 0.1875
- bias_query: bfloat16 [1024], P(('dp', 'blk')), may hold values from -3 to 3
- bias_value: bfloat16 [1024], P(('dp', 'blk')), may hold values from -3 to 3
- w_attn_out: bfloat16 [1024, 1024], P(('dp', 'blk')), may hold values from -1.5 to 1.5
- bias_attn_out: bfloat16 [1024], P(('dp', 'blk')), may hold values from -3 to 3
- ln1_gain: bfloat16 [1024], P(('dp', 'blk')), may hold values from 0.25 to 1.75
- ln1_shift: bfloat16 [1024], P(('dp', 'blk')), may hold values from -3 to 3
- w_ffn_in: bfloat16 [1024, 4096], P(('dp', 'blk')), may hold values from -0.1875 to 0.1875
- bias_ffn_in: bfloat16 [4096], P(('dp', 'blk')), may hold values from -3 to 3
- w_ffn_out: bfloat16 [4096, 1024], P(('dp', 'blk')), may hold values from -0.09375 to 0.09375
- bias_ffn_out: bfloat16 [1024], P(('dp', 'blk')), may hold values from -3 to 3
- ln2_gain: bfloat16 [1024], P(('dp', 'blk')), may hold values from 0.25 to 1.75
- ln2_shift: bfloat16 [1024], P(('dp', 'blk')), may hold values from -3 to 3
- cotangent: bfloat16 [4, 1024, 1024], P('dp', 'blk'), may hold values from -6 to 6
Outputs:
- outputs: bfloat16 [4, 1024, 1024], P('dp', 'blk')
- input_grad: bfloat16 [4, 1024, 1024], P('dp', 'blk')
- w_qkv_grad: float32 [1024, 3072], P(('dp', 'blk'))
- bias_query_grad: float32 [1024], P(('dp', 'blk'))
- bias_value_grad: float32 [1024], P(('dp', 'blk'))
- w_attn_out_grad: float32 [1024, 1024], P(('dp', 'blk'))
- bias_attn_out_grad: float32 [1024], P(('dp', 'blk'))
- ln1_gain_grad: float32 [1024], P(('dp', 'blk'))
- ln1_shift_grad: float32 [1024], P(('dp', 'blk'))
- w_ffn_in_grad: float32 [1024, 4096], P(('dp', 'blk'))
- bias_ffn_in_grad: float32 [4096], P(('dp', 'blk'))
- w_ffn_out_grad: float32 [4096, 1024], P(('dp', 'blk'))
- bias_ffn_out_grad: float32 [1024], P(('dp', 'blk'))
- ln2_gain_grad: float32 [1024], P(('dp', 'blk'))
- ln2_shift_grad: float32 [1024], P(('dp', 'blk'))
Inputs may be any that keep to these rules, and one draw needn't show every extreme that they name: `segments`: segment ids count the items of a row from 0 and never fall. Among the 2 rows on each index of dp, exactly one holds two items: the first of 960 positions, the second of the last 64. Every other row holds items that start at multiples of 128 and are 128 or 512 positions long. The first row of all that is not a two-item row holds only items of 128 positions. `pad_mask`: each item ends in a run of padding no longer than a quarter of its length (for the first item of a two-item row, than 16); every item has real tokens.
All inputs are finite; a program needn't handle non-finite values.
Results may differ from a plain program's by a relative error of at most 0.023.
Values may be sent and summed in bfloat16 or wider, within the bound.
A program may use at most 192 MiB of HBM per device.

v0:
```python
import math

import jax
import jax.numpy as jnp
from jax import lax
from jax.sharding import PartitionSpec as P

HEADS = 16
HEAD = 64
TSTEPS = 5000


EPSILON = 1e-05
NEGATIVE = -1e30


def time_features(timesteps, segments, model_width):
    item_count = timesteps.shape[1]
    numbers = jnp.arange(item_count, dtype=jnp.int32)
    picked = jnp.sum(
        jnp.where(segments[:, :, None] == numbers[None, None, :], timesteps[:, None, :], 0), axis=-1
    )
    half_width = model_width // 2
    frequency = jnp.exp(
        jnp.arange(half_width, dtype=jnp.float32) * (-math.log(10000.0) / half_width)
    )
    angles = picked.astype(jnp.float32)[..., None] * (100.0 / TSTEPS) * frequency
    return jnp.concatenate([jnp.sin(angles), jnp.cos(angles)], axis=-1)


def normalize(hidden):
    centered = hidden - jnp.mean(hidden, axis=-1, keepdims=True)
    inverse = lax.rsqrt(jnp.mean(centered * centered, axis=-1, keepdims=True) + EPSILON)
    return (centered * inverse, inverse)


def norm_backward(upstream, normed, inverse, gain):
    scaled = upstream * gain
    return inverse * (
        scaled
        - jnp.mean(scaled, axis=-1, keepdims=True)
        - normed * jnp.mean(scaled * normed, axis=-1, keepdims=True)
    )


def exact_gelu(values):
    return jax.nn.gelu(values, approximate=False)


def local(
    inputs,
    segments,
    pad_mask,
    timesteps,
    w_qkv,
    bias_query,
    bias_value,
    w_attn_out,
    bias_attn_out,
    ln1_gain,
    ln1_shift,
    w_ffn_in,
    bias_ffn_in,
    w_ffn_out,
    bias_ffn_out,
    ln2_gain,
    ln2_shift,
    cotangent,
):
    row_count, tok_count, model_width = inputs.shape
    flat_count = row_count * tok_count
    head_count = HEADS
    head_dim = HEAD
    scale = HEAD ** (-0.5)
    bf16 = jnp.bfloat16
    single = jnp.float32
    attn_full = (
        lax.all_gather(w_qkv, ("dp", "blk"), axis=0, tiled=True),
        lax.all_gather(bias_query, ("dp", "blk"), axis=0, tiled=True),
        lax.all_gather(bias_value, ("dp", "blk"), axis=0, tiled=True),
        lax.all_gather(w_attn_out, ("dp", "blk"), axis=0, tiled=True),
        lax.all_gather(bias_attn_out, ("dp", "blk"), axis=0, tiled=True),
        lax.all_gather(ln1_gain, ("dp", "blk"), axis=0, tiled=True),
        lax.all_gather(ln1_shift, ("dp", "blk"), axis=0, tiled=True),
    )
    qkv_weight, query_bias, value_bias, out_weight, out_bias, gain_one, shift_one = attn_full
    embedded = time_features(timesteps, segments, model_width)
    start_flat = (inputs.astype(single) + embedded).reshape(flat_count, model_width)
    start_low = start_flat.astype(bf16)
    projected = jnp.dot(start_low, qkv_weight, preferred_element_type=single)
    query_send = (
        (projected[:, :model_width] + query_bias.astype(single))
        .astype(bf16)
        .reshape(row_count, tok_count, model_width)
    )
    key_send = (
        projected[:, model_width : 2 * model_width]
        .astype(bf16)
        .reshape(row_count, tok_count, model_width)
    )
    value_send = (
        (projected[:, 2 * model_width :] + value_bias.astype(single))
        .astype(bf16)
        .reshape(row_count, tok_count, model_width)
    )
    query_heads = query_send.reshape(row_count, tok_count, head_count, head_dim)
    key_heads = key_send.reshape(row_count, tok_count, head_count, head_dim)
    value_heads = value_send.reshape(row_count, tok_count, head_count, head_dim)
    codes = jnp.where(pad_mask == 1, segments, -1)
    code_float = codes.astype(single)
    seg_float = segments.astype(single)
    code_send = codes.astype(bf16)
    seg_send = segments.astype(bf16)

    def split_heads(piece):
        return piece.reshape(piece.shape[0], piece.shape[1], head_count, head_dim)

    piece = (
        lax.all_gather(key_send, "blk", axis=1, tiled=True),
        lax.all_gather(value_send, "blk", axis=1, tiled=True),
        lax.all_gather(code_send, "blk", axis=1, tiled=True),
    )
    run_max = jnp.full((row_count, tok_count, head_count), NEGATIVE, single)
    piece_keys = split_heads(piece[0])
    piece_values = split_heads(piece[1])
    scores = (
        jnp.einsum("rqhe,rkhe->rqhk", query_heads, piece_keys, preferred_element_type=single)
        * scale
    )
    valid = seg_float[:, :, None, None] == piece[2].astype(single)[:, None, None, :]
    masked = jnp.where(valid, scores, NEGATIVE)
    new_max = jnp.maximum(run_max, jnp.max(masked, axis=-1))
    weights = jnp.where(valid, jnp.exp(masked - new_max[..., None]), 0.0)
    run_sum = jnp.sum(weights, axis=-1)
    run_acc = jnp.einsum(
        "rqhk,rkhe->rqhe", weights.astype(bf16), piece_values, preferred_element_type=single
    )
    run_max, run_sum, run_acc = (new_max, run_sum, run_acc)
    log_total = run_max + jnp.log(run_sum)
    attended = run_acc / run_sum[..., None]
    attended_low = attended.reshape(flat_count, model_width).astype(bf16)
    attn_branch = jnp.dot(
        attended_low, out_weight, preferred_element_type=single
    ) + out_bias.astype(single)
    normed_one, inverse_one = normalize(start_flat + attn_branch)
    gain_one_f = gain_one.astype(single)
    after_attn = normed_one * gain_one_f + shift_one.astype(single)
    ffn_full = (
        lax.all_gather(w_ffn_in, ("dp", "blk"), axis=0, tiled=True),
        lax.all_gather(bias_ffn_in, ("dp", "blk"), axis=0, tiled=True),
        lax.all_gather(w_ffn_out, ("dp", "blk"), axis=0, tiled=True),
        lax.all_gather(bias_ffn_out, ("dp", "blk"), axis=0, tiled=True),
        lax.all_gather(ln2_gain, ("dp", "blk"), axis=0, tiled=True),
        lax.all_gather(ln2_shift, ("dp", "blk"), axis=0, tiled=True),
    )
    in_weight, in_bias, down_weight, down_bias, gain_two, shift_two = ffn_full
    hidden_low = after_attn.astype(bf16)
    pre_act = jnp.dot(hidden_low, in_weight, preferred_element_type=single) + in_bias.astype(single)
    activated, gelu_pull = jax.vjp(exact_gelu, pre_act)
    activated_low = activated.astype(bf16)
    branch = jnp.dot(activated_low, down_weight, preferred_element_type=single) + down_bias.astype(
        single
    )
    normed_two, inverse_two = normalize(after_attn + branch)
    gain_two_f = gain_two.astype(single)
    outputs = (
        (normed_two * gain_two_f + shift_two.astype(single))
        .astype(bf16)
        .reshape(row_count, tok_count, model_width)
    )
    ffn_back = (
        lax.all_gather(w_ffn_in, ("dp", "blk"), axis=0, tiled=True),
        lax.all_gather(w_ffn_out, ("dp", "blk"), axis=0, tiled=True),
    )
    in_weight_back, down_weight_back = ffn_back
    upstream = cotangent.astype(single).reshape(flat_count, model_width)
    gain_two_grad = jnp.sum(upstream * normed_two, axis=0)
    shift_two_grad = jnp.sum(upstream, axis=0)
    second_grad = norm_backward(upstream, normed_two, inverse_two, gain_two_f)
    branch_grad = second_grad.astype(bf16)
    down_weight_grad = jnp.einsum(
        "tf,td->fd", activated_low, branch_grad, preferred_element_type=single
    )
    down_bias_grad = jnp.sum(branch_grad.astype(single), axis=0)
    act_grad = jnp.einsum("td,fd->tf", branch_grad, down_weight_back, preferred_element_type=single)
    pre_grad = gelu_pull(act_grad)[0].astype(bf16)
    in_weight_grad = jnp.einsum("td,tf->df", hidden_low, pre_grad, preferred_element_type=single)
    in_bias_grad = jnp.sum(pre_grad.astype(single), axis=0)
    hidden_grad = second_grad + jnp.einsum(
        "tf,df->td", pre_grad, in_weight_back, preferred_element_type=single
    )
    gain_one_grad = jnp.sum(hidden_grad * normed_one, axis=0)
    shift_one_grad = jnp.sum(hidden_grad, axis=0)
    first_grad = norm_backward(hidden_grad, normed_one, inverse_one, gain_one_f)
    ffn_grads = (
        lax.psum_scatter(in_weight_grad, ("dp", "blk"), scatter_dimension=0, tiled=True),
        lax.psum_scatter(in_bias_grad, ("dp", "blk"), scatter_dimension=0, tiled=True),
        lax.psum_scatter(down_weight_grad, ("dp", "blk"), scatter_dimension=0, tiled=True),
        lax.psum_scatter(down_bias_grad, ("dp", "blk"), scatter_dimension=0, tiled=True),
        lax.psum_scatter(gain_two_grad, ("dp", "blk"), scatter_dimension=0, tiled=True),
        lax.psum_scatter(shift_two_grad, ("dp", "blk"), scatter_dimension=0, tiled=True),
    )
    attn_back = (
        lax.all_gather(w_qkv, ("dp", "blk"), axis=0, tiled=True),
        lax.all_gather(w_attn_out, ("dp", "blk"), axis=0, tiled=True),
    )
    qkv_weight_back, out_weight_back = attn_back
    attn_grad_low = first_grad.astype(bf16)
    out_weight_grad = jnp.einsum(
        "td,te->de", attended_low, attn_grad_low, preferred_element_type=single
    )
    out_bias_grad = jnp.sum(attn_grad_low.astype(single), axis=0)
    attended_grad = jnp.einsum(
        "te,de->td", attn_grad_low, out_weight_back, preferred_element_type=single
    ).astype(bf16)
    grad_send = attended_grad.reshape(row_count, tok_count, model_width)
    grad_heads = grad_send.reshape(row_count, tok_count, head_count, head_dim)
    residue = jnp.sum(grad_heads.astype(single) * attended, axis=-1)
    stats_full = (
        lax.all_gather(log_total, "blk", axis=1, tiled=True),
        lax.all_gather(residue, "blk", axis=1, tiled=True),
    )
    log_full, residue_full = stats_full
    piece = (
        lax.all_gather(key_send, "blk", axis=1, tiled=True),
        lax.all_gather(value_send, "blk", axis=1, tiled=True),
        lax.all_gather(code_send, "blk", axis=1, tiled=True),
    )
    piece_keys = split_heads(piece[0])
    piece_values = split_heads(piece[1])
    scores = (
        jnp.einsum("rqhe,rkhe->rqhk", query_heads, piece_keys, preferred_element_type=single)
        * scale
    )
    valid = seg_float[:, :, None, None] == piece[2].astype(single)[:, None, None, :]
    probs = jnp.exp(jnp.where(valid, scores - log_total[..., None], NEGATIVE))
    prob_grad = jnp.einsum(
        "rqhe,rkhe->rqhk", grad_heads, piece_values, preferred_element_type=single
    )
    score_grad = (probs * (prob_grad - residue[..., None])).astype(bf16)
    query_grad = (
        jnp.einsum("rqhk,rkhe->rqhe", score_grad, piece_keys, preferred_element_type=single) * scale
    )
    piece = (
        lax.all_gather(query_send, "blk", axis=1, tiled=True),
        lax.all_gather(grad_send, "blk", axis=1, tiled=True),
        lax.all_gather(seg_send, "blk", axis=1, tiled=True),
    )
    piece_queries = split_heads(piece[0])
    piece_grads = split_heads(piece[1])
    scores = (
        jnp.einsum("rqhe,rkhe->rqhk", piece_queries, key_heads, preferred_element_type=single)
        * scale
    )
    valid = piece[2].astype(single)[:, :, None, None] == code_float[:, None, None, :]
    probs = jnp.exp(jnp.where(valid, scores - log_full[..., None], NEGATIVE))
    value_acc = jnp.einsum(
        "rqhk,rqhe->rkhe", probs.astype(bf16), piece_grads, preferred_element_type=single
    )
    prob_grad = jnp.einsum(
        "rqhe,rkhe->rqhk", piece_grads, value_heads, preferred_element_type=single
    )
    score_grad = (probs * (prob_grad - residue_full[..., None])).astype(bf16)
    key_acc = (
        jnp.einsum("rqhk,rqhe->rkhe", score_grad, piece_queries, preferred_element_type=single)
        * scale
    )
    query_low = query_grad.astype(bf16).reshape(flat_count, model_width)
    key_low = key_acc.astype(bf16).reshape(flat_count, model_width)
    value_low = value_acc.astype(bf16).reshape(flat_count, model_width)
    qkv_grad = jnp.concatenate([query_low, key_low, value_low], axis=1)
    qkv_weight_grad = jnp.einsum("td,tc->dc", start_low, qkv_grad, preferred_element_type=single)
    query_bias_grad = jnp.sum(query_low.astype(single), axis=0)
    value_bias_grad = jnp.sum(value_low.astype(single), axis=0)
    input_grad = (
        first_grad
        + jnp.einsum("tc,dc->td", qkv_grad, qkv_weight_back, preferred_element_type=single)
    ).astype(bf16)
    input_grad = input_grad.reshape(row_count, tok_count, model_width)
    attn_grads = (
        lax.psum_scatter(qkv_weight_grad, ("dp", "blk"), scatter_dimension=0, tiled=True),
        lax.psum_scatter(query_bias_grad, ("dp", "blk"), scatter_dimension=0, tiled=True),
        lax.psum_scatter(value_bias_grad, ("dp", "blk"), scatter_dimension=0, tiled=True),
        lax.psum_scatter(out_weight_grad, ("dp", "blk"), scatter_dimension=0, tiled=True),
        lax.psum_scatter(out_bias_grad, ("dp", "blk"), scatter_dimension=0, tiled=True),
        lax.psum_scatter(gain_one_grad, ("dp", "blk"), scatter_dimension=0, tiled=True),
        lax.psum_scatter(shift_one_grad, ("dp", "blk"), scatter_dimension=0, tiled=True),
    )
    return (
        outputs,
        input_grad,
        attn_grads[0],
        attn_grads[1],
        attn_grads[2],
        attn_grads[3],
        attn_grads[4],
        attn_grads[5],
        attn_grads[6],
        ffn_grads[0],
        ffn_grads[1],
        ffn_grads[2],
        ffn_grads[3],
        ffn_grads[4],
        ffn_grads[5],
    )


def solution(mesh):
    return jax.shard_map(
        local,
        mesh=mesh,
        in_specs=(
            P("dp", "blk", None),
            P("dp", "blk"),
            P("dp", "blk"),
            P("dp", None),
            P(("dp", "blk"), None),
            P(("dp", "blk")),
            P(("dp", "blk")),
            P(("dp", "blk"), None),
            P(("dp", "blk")),
            P(("dp", "blk")),
            P(("dp", "blk")),
            P(("dp", "blk"), None),
            P(("dp", "blk")),
            P(("dp", "blk"), None),
            P(("dp", "blk")),
            P(("dp", "blk")),
            P(("dp", "blk")),
            P("dp", "blk", None),
        ),
        out_specs=(
            P("dp", "blk", None),
            P("dp", "blk", None),
            P(("dp", "blk"), None),
            P(("dp", "blk")),
            P(("dp", "blk")),
            P(("dp", "blk"), None),
            P(("dp", "blk")),
            P(("dp", "blk")),
            P(("dp", "blk")),
            P(("dp", "blk"), None),
            P(("dp", "blk")),
            P(("dp", "blk"), None),
            P(("dp", "blk")),
            P(("dp", "blk")),
            P(("dp", "blk")),
        ),
        check_vma=False,
    )
```

profile of v0, /device:TPU:1, one launch (start us, length us, event | category | flops | bytes accessed | tf_op | source)
XLA Modules:
  0.0 1664.8 jit_solution(3668791763919056488)
XLA Ops:
  10.9 72.1 %all-gather.12.cloned.1.call-done = bf16[1024,3072]{1,0:T(8,128)(2,1)} async-done(((bf16[32,3072]{1,0:T(8,128)(2,1)}), bf16[1024,3072]{1,0:T(8,128)(2,1)}) %all-gather.12.cloned.1.call-update) | async-done | bytes 6291472 | tf_op jit(solution)/shard_map/all_gather | solution.py:78
  89.5 39.2 %all-reduce.18 = (bf16[1024]{0:T(1024)(128)(2,1)S(1)}, bf16[1024]{0:T(1024)(128)(2,1)S(1)}, bf16[1024]{0:T(1024)(128)(2,1)S(1)}, bf16[1024]{0:T(1024)(128)(2,1)S...) all-reduce(bf16[1024]{0:T(1024)(128)(2,1)S(1)} %dynamic-update-slic, ...), channel_id=1, replica_groups=mesh['dp'=2,'blk'=16] {'dp','blk'}, use_global_device_ids=true, to_apply=%add | all-reduce | flops 8192 | bytes 32768
  131.4 68.3 %all-gather.1 = bf16[32,1,128]{2,1,0:T(2,128)(2,1)S(1)} all-gather(bf16[1,1,128]{2,1,0:T(2,128)(2,1)S(1)} %bitcast.192), channel_id=1, replica_groups=mesh['dp'=2,'blk'=16] {'dp','blk'}, dimensions={0}, use_global_device_ids=true | all-gather | bytes 8448 | tf_op jit(solution)/shard_map/all_gather | solution.py:150
  200.3 28.5 %all-gather = bf16[16,64,2]{1,2,0:T(2,128)(2,1)S(1)} all-gather(bf16[1,64,2]{1,2,0:T(2,128)(2,1)S(1)} %get-tuple-element.50), channel_id=1, replica_groups=mesh['dp'=2,'blk'=16] {'blk'}, dimensions={0}, use_global_device_ids=true | all-gather | bytes 4352 | tf_op jit(solution)/shard_map/all_gather | solution.py:121
  246.5 6.7 copy.116
  253.2 8.3 fusion.113
  262.4 35.8 %all-gather.18.cloned.1.call-done = bf16[1024,1024]{1,0:T(8,128)(2,1)} async-done(((bf16[32,1024]{1,0:T(8,128)(2,1)}), bf16[1024,1024]{1,0:T(8,128)(2,1)}) %all-gather.18.cloned.1.call-update) | async-done | bytes 2097168 | tf_op jit(solution)/shard_map/all_gather | solution.py:81
  300.5 76.8 %all-gather.20.cloned.1.call-done = bf16[1024,4096]{1,0:T(8,128)(2,1)} async-done(((bf16[32,4096]{1,0:T(8,128)(2,1)}), bf16[1024,4096]{1,0:T(8,128)(2,1)}) %all-gather.20.cloned.1.call-update) | async-done | bytes 8388624 | tf_op jit(solution)/shard_map/all_gather | solution.py:149
  383.4 72.8 %all-gather.22.cloned.1.call-done = bf16[4096,1024]{1,0:T(8,128)(2,1)} async-done(((bf16[128,1024]{1,0:T(8,128)(2,1)}), bf16[4096,1024]{1,0:T(8,128)(2,1)}) %all-gather.22.cloned.1.call-update) | async-done | bytes 8388624 | tf_op jit(solution)/shard_map/all_gather | solution.py:151
  456.2 9.7 fusion.115
  468.5 8.3 convert_reduce_fusion
  486.2 31.1 %all-gather.2 = bf16[16,64,2]{1,2,0:T(2,128)(2,1)S(1)} all-gather(bf16[1,64,2]{1,2,0:T(2,128)(2,1)S(1)} %copy-done.27), channel_id=1, replica_groups=mesh['dp'=2,'blk'=16] {'blk'}, dimensions={0}, use_global_device_ids=true | all-gather | bytes 4352 | tf_op jit(solution)/shard_map/all_gather | solution.py:247
  524.8 11.3 convert_reduce_fusion.2
  537.9 43.0 %all_gather.90 = f32[2,1024,16]{2,0,1:T(2,128)} all-gather(f32[2,64,16]{2,0,1:T(2,128)S(1)} %copy.131), channel_id=1, replica_groups=mesh['dp'=2,'blk'=16] {'blk'}, dimensions={1}, use_global_device_ids=true | all-gather | bytes 139264 | tf_op jit(solution)/shard_map/all_gather | solution.py:221
  582.9 47.2 %all_gather.88 = f32[2,1024,16]{2,0,1:T(2,128)} all-gather(f32[2,64,16]{2,0,1:T(2,128)S(1)} %copy.127), channel_id=1, replica_groups=mesh['dp'=2,'blk'=16] {'blk'}, dimensions={1}, use_global_device_ids=true | all-gather | bytes 139264 | tf_op jit(solution)/shard_map/all_gather | solution.py:220
  637.7 6.8 fusion.85
  650.9 10.8 fusion.59
  665.3 7.2 convert_reduce_fusion.1
  683.4 8.2 fusion.109
  692.7 11.0 fusion.94
  704.5 60.1 %all-reduce.17 = (f32[1024]{0:T(1024)S(1)}, f32[1024]{0:T(1024)S(1)}, f32[1024]{0:T(1024)S(1)}, f32[1024]{0:T(1024)S(1)}, f32[1024]{0:T(1024)S(1)}, /*index=5*/f...) all-reduce(f32[1024]{0:T(1024)S(1)} %reduce_sum.196, ...), channel_id=3, replica_groups=mesh['dp'=2,'blk'=16] {'dp','blk'}, use_global_device_ids=true, to_apply=%region_14.15.clone | all-reduce | flops 12288 | bytes 98304
  776.8 156.8 %reduce-scatter.5.cloned.1.call-done = f32[32,3072]{1,0:T(8,128)} async-done(((f32[1024,3072]{1,0:T(8,128)}), f32[32,3072]{1,0:T(8,128)}) %reduce-scatter.5.cloned.1.call-update) | async-done | bytes 393232 | tf_op jit(solution)/shard_map/reduce_scatter | solution.py:281
  933.6 361.0 %reduce-scatter.9.cloned.1.call-done = f32[32,4096]{1,0:T(8,128)} async-done(((f32[1024,4096]{1,0:T(8,128)}), f32[32,4096]{1,0:T(8,128)}) %reduce-scatter.9.cloned.1.call-update) | async-done | bytes 524304 | tf_op jit(solution)/shard_map/reduce_scatter | solution.py:196
  1294.6 362.9 %reduce-scatter.11.cloned.1.call-done = f32[128,1024]{1,0:T(8,128)} async-done(((f32[4096,1024]{1,0:T(8,128)}), f32[128,1024]{1,0:T(8,128)}) %reduce-scatter.11.cloned.1.call-update) | async-done | bytes 524304 | tf_op jit(solution)/shard_map/reduce_scatter | solution.py:198
  (213 shorter events, 105.6 us)
Async XLA Ops:
  7.2 75.8 %all-gather.12.cloned.1.call-start = ((), (), s32[]{:S(2)}) async-start(), calls=%async_computation.4 | async-start | bytes 6488064 | tf_op jit(solution)/shard_map/all_gather | solution.py:78
  7.9 222.4 %all-gather.16.cloned.1.call-start = ((), (), s32[]{:S(2)}) async-start(), calls=%async_computation.6 | async-start | bytes 4456448 | tf_op jit(solution)/shard_map/all_gather | solution.py:119
  10.8 76.8 %copy-start.31 = (bf16[32]{0:T(256)(128)(2,1)S(1)}, bf16[32]{0:T(256)(128)(2,1)}, u32[]{:S(2)}) copy-start(bf16[32]{0:T(256)(128)(2,1)} %param.24) | copy-start | bytes 196
  10.8 77.1 %copy-start.32 = (bf16[32]{0:T(256)(128)(2,1)S(1)}, bf16[32]{0:T(256)(128)(2,1)}, u32[]{:S(2)}) copy-start(bf16[32]{0:T(256)(128)(2,1)} %param.23) | copy-start | bytes 196
  10.8 77.3 %copy-start.33 = (bf16[32]{0:T(256)(128)(2,1)S(1)}, bf16[32]{0:T(256)(128)(2,1)}, u32[]{:S(2)}) copy-start(bf16[32]{0:T(256)(128)(2,1)} %param.26) | copy-start | bytes 196
  10.8 77.5 %copy-start.34 = (bf16[32]{0:T(256)(128)(2,1)S(1)}, bf16[32]{0:T(256)(128)(2,1)}, u32[]{:S(2)}) copy-start(bf16[32]{0:T(256)(128)(2,1)} %param.32) | copy-start | bytes 196
  10.9 77.8 %copy-start.35 = (bf16[32]{0:T(256)(128)(2,1)S(1)}, bf16[32]{0:T(256)(128)(2,1)}, u32[]{:S(2)}) copy-start(bf16[32]{0:T(256)(128)(2,1)} %param.28) | copy-start | bytes 196
  10.9 78.0 %copy-start.36 = (bf16[32]{0:T(256)(128)(2,1)S(1)}, bf16[32]{0:T(256)(128)(2,1)}, u32[]{:S(2)}) copy-start(bf16[32]{0:T(256)(128)(2,1)} %param.27) | copy-start | bytes 196
  10.9 78.2 %copy-start.37 = (bf16[32]{0:T(256)(128)(2,1)S(1)}, bf16[32]{0:T(256)(128)(2,1)}, u32[]{:S(2)}) copy-start(bf16[32]{0:T(256)(128)(2,1)} %param.34) | copy-start | bytes 196
  10.9 78.4 %copy-start.38 = (bf16[32]{0:T(256)(128)(2,1)S(1)}, bf16[32]{0:T(256)(128)(2,1)}, u32[]{:S(2)}) copy-start(bf16[32]{0:T(256)(128)(2,1)} %param.33) | copy-start | bytes 196
  86.8 112.9 %copy-start.26 = (s32[2,64]{1,0:T(2,128)S(1)}, s32[2,64]{1,0:T(2,128)}, u32[]{:S(2)}) copy-start(s32[2,64]{1,0:T(2,128)} %param.19) | copy-start | bytes 1540
  86.8 112.9 %copy-start.28 = (s32[2,64]{1,0:T(2,128)S(1)}, s32[2,64]{1,0:T(2,128)}, u32[]{:S(2)}) copy-start(s32[2,64]{1,0:T(2,128)} %param.20) | copy-start | bytes 1540
  86.8 142.1 %copy-start.2 = (bf16[2,64,1024]{2,1,0:T(8,128)(2,1)S(1)}, bf16[2,64,1024]{2,1,0:T(8,128)(2,1)}, u32[]{:S(2)}) copy-start(bf16[2,64,1024]{2,1,0:T(8,128)(2,1)} %param.35) | copy-start | bytes 786436
  87.6 158.9 %all-gather.14.cloned.1.call-start = ((), (), s32[]{:S(2)}) async-start(), calls=%async_computation.5 | async-start | bytes 4456448 | tf_op jit(solution)/shard_map/all_gather | solution.py:120
  129.6 100.6 %copy-start.4 = (bf16[128,1024]{1,0:T(8,128)(2,1)}, bf16[128,1024]{1,0:T(8,128)(2,1)S(1)}, u32[]{:S(2)}) copy-start(bf16[128,1024]{1,0:T(8,128)(2,1)S(1)} %get-tuple-element.44) | copy-start | bytes 786436
  129.6 168.5 %all-gather.18.cloned.1.call-start = ((), (), s32[]{:S(2)}) async-start(), calls=%async_computation.7 | async-start | bytes 2162688 | tf_op jit(solution)/shard_map/all_gather | solution.py:81
  130.2 247.1 %all-gather.20.cloned.1.call-start = ((), (), s32[]{:S(2)}) async-start(), calls=%async_computation.8 | async-start | bytes 8650752 | tf_op jit(solution)/shard_map/all_gather | solution.py:149
  130.8 325.4 %all-gather.22.cloned.1.call-start = ((), (), s32[]{:S(2)}) async-start(), calls=%async_computation.9 | async-start | bytes 8650752 | tf_op jit(solution)/shard_map/all_gather | solution.py:151
  131.3 500.1 %all-gather.24.cloned.1.call-start = ((), (), s32[]{:S(2)}) async-start(), calls=%async_computation.10 | async-start | bytes 4456448 | tf_op jit(solution)/shard_map/all_gather | solution.py:245
  230.2 414.3 %all-gather.26.cloned.1.call-start = ((), (), s32[]{:S(2)}) async-start(), calls=%async_computation.11 | async-start | bytes 4456448 | tf_op jit(solution)/shard_map/all_gather | solution.py:246
  482.8 294.0 %reduce-scatter.7.cloned.1.call-start = ((), (), s32[]{:S(2)}) async-start(), calls=%async_computation.13 | async-start | bytes 4325376 | tf_op jit(solution)/shard_map/reduce_scatter | solution.py:284
  485.6 448.1 %reduce-scatter.5.cloned.1.call-start = ((), (), s32[]{:S(2)}) async-start(), calls=%async_computation.12 | async-start | bytes 12976128 | tf_op jit(solution)/shard_map/reduce_scatter | solution.py:281
  683.1 611.5 %reduce-scatter.9.cloned.1.call-start = ((), (), s32[]{:S(2)}) async-start(), calls=%async_computation.14 | async-start | bytes 17301504 | tf_op jit(solution)/shard_map/reduce_scatter | solution.py:196
  691.6 965.9 %reduce-scatter.11.cloned.1.call-start = ((), (), s32[]{:S(2)}) async-start(), calls=%async_computation.15 | async-start | bytes 17301504 | tf_op jit(solution)/shard_map/reduce_scatter | solution.py:198
  (29 other events, 272.7 us)
Sparse Core Ops, SparseCore 0:
  10.9 72.0 all-gather.11
  87.7 73.1 all-gather.15
  164.3 74.4 all-gather.13
  241.5 56.6 all-gather.17
  300.9 76.3 all-gather.19
  380.0 76.1 all-gather.21
  459.0 73.0 all-gather.23
  534.8 92.4 all-gather.25
  630.1 146.5 reduce-scatter.6
  783.2 150.3 reduce-scatter.4
  936.6 357.9 reduce-scatter.8
  1297.4 360.0 reduce-scatter.10
where the time goes:
time: 1680 us; the launch traced here: 1660 us
  waiting for transfers between devices  1140 us (68%)
  blocking collectives  317 us (19%)
  matrix products  118 us (7%)
  local copies, waits for them, and re-layouts  58.6 us (3%)
    reduce_scatter x1, waiting for transfers between devices, local(): lax.psum_scatter(down_weight_grad, ('dp', 'blk'), scatter_dimension=0, ti...  363 us
    reduce_scatter x1, waiting for transfers between devices, local(): lax.psum_scatter(in_weight_grad, ('dp', 'blk'), scatter_dimension=0, tile...  361 us
    reduce_scatter x1, waiting for transfers between devices, local(): lax.psum_scatter(qkv_weight_grad, ('dp', 'blk'), scatter_dimension=0, til...  157 us
    unnamed x2, blocking collectives  99.3 us
    all_gather x1, waiting for transfers between devices, local(): lax.all_gather(w_ffn_in, ('dp', 'blk'), axis=0, tiled=True)  76.8 us
    all_gather x1, waiting for transfers between devices, local(): lax.all_gather(w_ffn_out, ('dp', 'blk'), axis=0, tiled=True)  72.8 us
    all_gather x1, waiting for transfers between devices, local(): lax.all_gather(w_qkv, ('dp', 'blk'), axis=0, tiled=True)  72.1 us
    all_gather x1, blocking collectives, local(): lax.all_gather(bias_ffn_in, ('dp', 'blk'), axis=0, tiled=True)  68.3 us
  transfers between devices with their start and end apart: 12, of which 8 were waited for; matrix products, arithmetic and copies ran while one was open for 11% of the time, Pallas kernels for 0%

commit v1 on v0

--- a/solution.py
+++ b/solution.py
@@ -1,8 +1,11 @@
+import functools
 import math
 
 import jax
 import jax.numpy as jnp
 from jax import lax
+from jax.experimental import pallas as pl
+from jax.experimental.pallas import tpu as pltpu
 from jax.sharding import PartitionSpec as P
 
 HEADS = 16
@@ -305,9 +308,907 @@
     )
 
 
+MESH = pl.DeviceIdType.MESH
+PLANE = 4
+PLANES = 4
+TILE = 256
+BF16 = jnp.bfloat16
+F32 = jnp.float32
+
+
+def mm(left, right, left_dim=1, right_dim=0):
+    return lax.dot_general(
+        left, right, (((left_dim,), (right_dim,)), ((), ())), preferred_element_type=F32
+    )
+
+
+def wide_slice(start, size, step):
+    return pl.ds(pl.multiple_of(start, step), size)
+
+
+class Names:
+    pass
+
+
+class Labels:
+    def __getattr__(self, name):
+        return name
+
+
+N = Labels()
+SEND, RECV = 0, 1
+
+
+def scratch_plan(tok, model, hidden):
+    chunk = 2 * tok
+    toks = PLANE * chunk
+    keys = 2 * toks
+    wid = model // PLANE
+    units = hidden // PLANE
+    rows = model // 32
+    zrows = PLANE * rows
+    half = PLANES * zrows
+    return dict(
+        xin=((chunk, model), BF16),
+        cin=((chunk, model), BF16),
+        tbl=((8, model), F32),
+        inf_in=((2, 8, 128), F32),
+        inf=((8, 8, 128), F32),
+        smalls=((2, PLANES, PLANE, 16, 128), BF16),
+        vec=((16, model), F32),
+        ffb=((16, units), F32),
+        wqkv=((model, 3 * wid), BF16),
+        wo=((model, model), BF16),
+        win=((model, units), BF16),
+        wfo=((units, model), BF16),
+        sres=((chunk, model), F32),
+        slow=((toks, model), BF16),
+        q=((toks, wid), BF16),
+        kv=((keys, 2 * wid), BF16),
+        bias=((toks, keys), F32),
+        att=((toks, wid), F32),
+        lse=((4, toks, 1), F32),
+        attl=((toks, wid), BF16),
+        attx=((chunk, model), BF16),
+        n1=((chunk, model), F32),
+        inv1=((chunk, 1), F32),
+        aft=((chunk, model), F32),
+        hid=((toks, model), BF16),
+        pre=((toks, units), F32),
+        act=((toks, units), BF16),
+        fs=((PLANE, chunk, model), BF16),
+        fr=((PLANE, chunk, model), BF16),
+        own=((chunk, model), F32),
+        outl=((chunk, model), BF16),
+        outr=((2, tok, model), BF16),
+        second=((chunk, model), F32),
+        bg=((toks, model), BF16),
+        pg=((toks, units), BF16),
+        first=((chunk, model), F32),
+        agl=((chunk, model), BF16),
+        ado=((chunk, model), BF16),
+        do=((toks, wid), BF16),
+        dq=((toks, wid), F32),
+        dk=((keys, wid), F32),
+        dv=((keys, wid), F32),
+        dkvs=((toks, 2 * wid), BF16),
+        dkvr=((toks, 2 * wid), BF16),
+        dqkv=((toks, 3 * wid), BF16),
+        igl=((chunk, model), BF16),
+        igr=((2, tok, model), BF16),
+        gfo_s=((half, model), BF16),
+        gfo_r=((half, model), BF16),
+        gfo_o=((zrows, model), F32),
+        gfo_zs=((4, zrows, model), BF16),
+        gfo_zr=((4, zrows, model), BF16),
+        gwi_s=((half, units), BF16),
+        gwi_r=((half, units), BF16),
+        gwi_o=((zrows, units), F32),
+        gwi_zs=((4, zrows, units), BF16),
+        gwi_zr=((4, zrows, units), BF16),
+        gwi_p=((zrows, units), BF16),
+        gwi_pr=((4, rows, units), BF16),
+        gqk_s=((half, 3 * wid), BF16),
+        gqk_r=((half, 3 * wid), BF16),
+        gqk_o=((zrows, 3 * wid), F32),
+        gqk_zs=((4, zrows, 3 * wid), BF16),
+        gqk_zr=((4, zrows, 3 * wid), BF16),
+        gqk_p=((zrows, 3 * wid), BF16),
+        gqk_pr=((4, rows, 3 * wid), BF16),
+        gwo_s=((half, model), BF16),
+        gwo_r=((half, model), BF16),
+        gwo_o=((half, model), F32),
+        gwo_p=((half, model), BF16),
+        gwo_pr=((4, PLANES, rows, model), BF16),
+        gwo_zs=((4, rows, model), BF16),
+        gwo_zr=((4, rows, model), BF16),
+        smg=((16, model), F32),
+        sma=((8, 16, 128), F32),
+        smb=((16, 128), F32),
+        smb_r=((4, 16, 128), F32),
+    )
+
+
+N_SEND = 64
+N_RECV = 160
+
+
+def fused(plan, tok, model, hidden, *refs):
+    (x_ref, cot_ref, table_ref, small_ref, info_ref, wqkv_ref, wo_ref, win_ref, wfo_ref) = refs[:9]
+    (out_ref, ig_ref, dwqkv_ref, dwo_ref, dwin_ref, dwfo_ref, sg_ref) = refs[9:16]
+    s = Names()
+    for name, ref in zip(plan, refs[16:]):
+        setattr(s, name, ref)
+    send_pool, recv_pool = refs[16 + len(plan):]
+
+    chunk = 2 * tok
+    toks = PLANE * chunk
+    keys = 2 * toks
+    wid = model // PLANE
+    units = hidden // PLANE
+    rows = model // 32
+    zrows = PLANE * rows
+    half = PLANES * zrows
+    heads = wid // HEAD
+    frows = hidden // 32
+
+    c = lax.axis_index("dp")
+    b = lax.axis_index("blk")
+    z = b // PLANE
+    p = b % PLANE
+    y, x = p // 2, p % 2
+    other = 1 - c
+    plane_peers = [p, y * 2 + (1 - x), (1 - y) * 2 + x, PLANE - 1 - p]
+    z_peers = [(z + k) % PLANES for k in range(PLANES)]
+    z_back = [(z + PLANES - k) % PLANES for k in range(PLANES)]
+
+    def dev(cc, zz, pp):
+        return {"dp": cc, "blk": zz * PLANE + pp}
+
+    used = ({}, {})
+
+    def sem(kind, name):
+        table = used[kind]
+        if name not in table:
+            table[name] = len(table)
+            assert table[name] < (N_SEND, N_RECV)[kind]
+        return (send_pool, recv_pool)[kind].at[table[name]]
+
+    pending = []
+
+    def remote(src, dst, send_name, recv_name, target):
+        pltpu.make_async_remote_copy(
+            src_ref=src,
+            dst_ref=dst,
+            send_sem=sem(SEND, send_name),
+            recv_sem=sem(RECV, recv_name),
+            device_id=target,
+            device_id_type=MESH,
+        ).start()
+
+    def sent(ref, send_name, cond=None):
+        pending.append((ref, send_name, cond))
+
+    def flush_sent():
+        for ref, send_name, cond in pending:
+            def one():
+                handle = sem(SEND, send_name)
+                pltpu.make_async_copy(ref, ref, handle).wait()
+            if cond is None:
+                one()
+            else:
+                pl.when(cond)(one)
+        pending.clear()
+
+    def arrived(ref, recv_name):
+        pltpu.make_async_copy(ref, ref, sem(RECV, recv_name)).wait()
+
+    def maybe_local(src, dst, send_name, recv_name, target, is_self):
+        send_handle = sem(SEND, send_name)
+        recv_handle = sem(RECV, recv_name)
+
+        @pl.when(is_self)
+        def _():
+            pltpu.make_async_copy(src, dst, recv_handle).start()
+
+        @pl.when(jnp.logical_not(is_self))
+        def _():
+            pltpu.make_async_remote_copy(
+                src_ref=src, dst_ref=dst, send_sem=send_handle, recv_sem=recv_handle,
+                device_id=target, device_id_type=MESH,
+            ).start()
+
+        sent(src, send_name, jnp.logical_not(is_self))
+
+    barrier = pltpu.get_barrier_semaphore()
+    greeted = [dev(c, z, plane_peers[k]) for k in (1, 2, 3)]
+    greeted += [dev(c, z_peers[k], p) for k in (1, 2, 3)]
+    greeted += [dev(other, z_peers[k], p) for k in (0, 1, 2, 3)]
+    for target in greeted:
+        pl.semaphore_signal(barrier, inc=1, device_id=target, device_id_type=MESH)
+    pl.semaphore_wait(barrier, len(greeted))
+
+    home = z // 2
+    slot = z % 2
+    for i in range(2):
+        plane_of = 2 * c + i
+        is_self = jnp.logical_and(home == c, plane_of == z)
+        target = dev(home, plane_of, p)
+        maybe_local(x_ref.at[i], s.xin.at[wide_slice(slot * tok, tok, tok)], (N.x, i), N.x, target, is_self)
+        maybe_local(info_ref.at[i], s.inf_in.at[slot], (N.i, i), N.i, target, is_self)
+
+    table_here = home == c
+
+    @pl.when(table_here)
+    def _():
+        remote(table_ref.at[slot], s.tbl, N.tbl, N.tbl, dev(other, z, p))
+        s.tbl[...] = table_ref[slot]
+
+    wrow = (c * 16 + z * 4 + p) * rows
+    for t in range(3):
+        pltpu.make_async_copy(
+            wqkv_ref.at[:, wide_slice(t * model + p * wid, wid, wid)],
+            s.wqkv.at[wide_slice(wrow, rows, rows), pl.ds(t * wid, wid)],
+            sem(RECV, N.wq0),
+        ).start()
+    for k in (3, 1, 2):
+        pp = plane_peers[k]
+        for t in range(3):
+            remote(
+                wqkv_ref.at[:, wide_slice(t * model + pp * wid, wid, wid)],
+                s.wqkv.at[wide_slice(wrow, rows, rows), pl.ds(t * wid, wid)],
+                (N.wq1, k), (N.wq1, k), dev(c, z, pp),
+            )
+        sent(s.wqkv.at[pl.ds(0, rows)], (N.wq1, k))
+
+    s.smalls[c, z, p] = small_ref[...]
+    for k in (1, 2, 3):
+        remote(small_ref, s.smalls.at[c, z, p], N.smz, (N.smz, k), dev(c, z_peers[k], p))
+    sent(s.smalls.at[0, 0, pl.ds(0, 3)], N.smz)
+
+    pltpu.make_async_copy(wo_ref, s.wo.at[wide_slice(wrow, rows, rows)], sem(RECV, N.wo0)).start()
+    for k in (1, 2, 3):
+        remote(wo_ref, s.wo.at[wide_slice(wrow, rows, rows)], N.woz, (N.woz, k), dev(c, z_peers[k], p))
+    sent(s.wo.at[pl.ds(0, 3 * rows)], N.woz)
+
+    arrived(s.wqkv.at[pl.ds(0, rows)], N.wq0)
+    for k in (1, 2, 3):
+        arrived(s.wqkv.at[pl.ds(0, rows)], (N.wq1, k))
+    zrow = c * half + z * zrows
+    wq_block = s.wqkv.at[wide_slice(zrow, zrows, zrows)]
+    for k in (1, 2, 3):
+        remote(wq_block, wq_block, N.wq2, (N.wq2, k), dev(c, z_peers[k], p))
+    sent(s.wqkv.at[pl.ds(0, 3 * zrows)], N.wq2)
+    remote(wq_block, wq_block, N.wq3, N.wq3, dev(other, z, p))
+
+    arrived(s.inf_in, N.i)
+    info_own = s.inf_in[0] + s.inf_in[1]
+    s.inf[c * 4 + p] = info_own
+    for k in (1, 2, 3):
+        blk_ref = s.inf.at[c * 4 + p]
+        remote(blk_ref, blk_ref, N.inf, (N.inf, k), dev(c, z, plane_peers[k]))
+    sent(s.inf.at[pl.ds(0, 3)], N.inf)
+
+    @pl.when(jnp.logical_not(table_here))
+    def _():
+        arrived(s.tbl, N.tbl)
+
+    arrived(s.xin, N.x)
+    items = lax.broadcasted_iota(jnp.int32, (8, chunk), 0).astype(F32)
+    onehot = jnp.where(info_own[0:1, :] == items + 1.0, 1.0, 0.0)
+    embedded = lax.dot_general(
+        onehot, s.tbl[...], (((0,), (0,)), ((), ())), precision=lax.Precision.HIGHEST,
+        preferred_element_type=F32,
+    )
+    start_res = s.xin[...].astype(F32) + embedded
+    s.sres[...] = start_res
+    prow = p * chunk
+    own_rows = wide_slice(prow, chunk, chunk)
+    s.slow[own_rows, :] = start_res.astype(BF16)
+
+    def plane_gather(ref, name):
+        for k in (1, 2, 3):
+            block = ref.at[own_rows]
+            remote(block, block, name, (name, k), dev(c, z, plane_peers[k]))
+        sent(ref.at[pl.ds(0, 3 * chunk)], name)
+
+    plane_gather(s.slow, N.slow)
+
+    for i in range(2):
+        plane_of = 2 * c + i
+        is_self = jnp.logical_and(home == c, plane_of == z)
+        target = dev(home, plane_of, p)
+        maybe_local(cot_ref.at[i], s.cin.at[wide_slice(slot * tok, tok, tok)], (N.c, i), N.c, target, is_self)
+    for g in range(8):
+        pltpu.make_async_copy(
+            win_ref.at[:, wide_slice(g * 4 * frows + p * frows, frows, frows)],
+            s.win.at[wide_slice(wrow, rows, rows), pl.ds(g * frows, frows)],
+            sem(RECV, N.wi0),
+        ).start()
+    for k in (3, 1, 2):
+        pp = plane_peers[k]
+        for g in range(8):
+            remote(
+                win_ref.at[:, wide_slice(g * 4 * frows + pp * frows, frows, frows)],
+                s.win.at[wide_slice(wrow, rows, rows), pl.ds(g * frows, frows)],
+                (N.wi1, k), (N.wi1, k), dev(c, z, pp),
+            )
+        sent(s.win.at[pl.ds(0, rows)], (N.wi1, k))
+    for k in (1, 2, 3):
+        arrived(s.smalls.at[0, 0, 0], (N.smz, k))
+    for k in (1, 2, 3):
+        for zz in range(PLANES):
+            ref = s.smalls.at[c, zz, p]
+            remote(ref, ref, N.smp, (N.smp, k), dev(c, z, plane_peers[k]))
+    sent(s.smalls.at[0, pl.ds(0, 3)], N.smp)
+    for k in (1, 2, 3):
+        arrived(s.inf.at[0], (N.inf, k))
+    inf_half = s.inf.at[wide_slice(c * 4, 4, 4)]
+    remote(inf_half, inf_half, N.infs, N.infs, dev(other, z, p))
+    sent(inf_half, N.infs)
+    for k in (1, 2, 3):
+        arrived(s.smalls.at[0, 0], (N.smp, k))
+    remote(s.smalls.at[c], s.smalls.at[c], N.sms, N.sms, dev(other, z, p))
+    sent(s.smalls.at[0], N.sms)
+    arrived(wo_ref, N.wo0)
+    for k in (1, 2, 3):
+        arrived(wo_ref, (N.woz, k))
+    arrived(s.win.at[pl.ds(0, rows)], N.wi0)
+    for k in (1, 2, 3):
+        arrived(s.win.at[pl.ds(0, rows)], (N.wi1, k))
+    wi_block = s.win.at[wide_slice(zrow, zrows, zrows)]
+    for k in (1, 2, 3):
+        remote(wi_block, wi_block, N.wi2, (N.wi2, k), dev(c, z_peers[k], p))
+    sent(s.win.at[pl.ds(0, 3 * zrows)], N.wi2)
+    remote(wi_block, wi_block, N.wi3, N.wi3, dev(other, z, p))
+    fblock = (c * 4 + z) * frows
+    f_ref = s.wfo.at[wide_slice(fblock, frows, frows)]
+    pltpu.make_async_copy(wfo_ref, f_ref, sem(RECV, N.wf0)).start()
+    for k in (1, 2, 3):
+        remote(wfo_ref, f_ref, N.wf2, (N.wf2, k), dev(c, z_peers[k], p))
+    sent(s.wfo.at[pl.ds(0, 3 * frows)], N.wf2)
+    remote(wfo_ref, f_ref, N.wf3, N.wf3, dev(other, z, p))
+
+    arrived(s.smalls.at[0], N.sms)
+    pieces = s.smalls[...].reshape(512, 128)
+    lane = lax.broadcasted_iota(jnp.int32, (128, model), 1)
+    sub = lax.broadcasted_iota(jnp.int32, (128, model), 0)
+    spread = jnp.where(lane % rows == sub, 1.0, 0.0).astype(BF16)
+    laid = mm(pieces, spread)
+    lane2 = lax.broadcasted_iota(jnp.int32, (512, model), 1)
+    sub2 = lax.broadcasted_iota(jnp.int32, (512, model), 0)
+    laid = jnp.where(lane2 // rows == sub2 // 16, laid, 0.0)
+    s.vec[...] = jnp.sum(laid.reshape(32, 16, model), axis=0)
+    for g in range(8):
+        s.ffb[:, pl.ds(g * frows, frows)] = s.smalls[g // 4, g % 4, p].astype(F32)
+    arrived(inf_half, N.infs)
+    code_hot = []
+    for g in range(8):
+        code_hot.append(jnp.where(s.inf[g][1:2, :] == items + 1.0, 1.0, 0.0))
+    seg_hot = []
+    for g in range(4):
+        seg_hot.append(jnp.where(s.inf[c * 4 + g][0:1, :] == items + 1.0, 1.0, 0.0))
+    code_hot = jnp.concatenate(code_hot, axis=1)
+    seg_hot = jnp.concatenate(seg_hot, axis=1)
+    s.bias[...] = (mm(seg_hot, code_hot, 0, 0) - 1.0) * -NEGATIVE
+
+    for k in (1, 2, 3):
+        arrived(s.wqkv.at[pl.ds(0, zrows)], (N.wq2, k))
+        block = s.wqkv.at[wide_slice(c * half + z_back[k] * zrows, zrows, zrows)]
+        remote(block, block, N.wq3, N.wq3, dev(other, z, p))
+    sent(s.wqkv.at[pl.ds(0, half)], N.wq3)
+    for zz in range(PLANES):
+        block = s.wo.at[wide_slice((c * 16 + zz * 4 + p) * rows, rows, rows)]
+        for k in (1, 2, 3):
+            remote(block, block, N.wop, (N.wop, k), dev(c, z, plane_peers[k]))
+    sent(s.wo.at[pl.ds(0, 3 * PLANES * rows)], N.wop)
+    arrived(s.wqkv.at[pl.ds(0, half)], N.wq3)
+
+    q_bias = s.vec[0:1, wide_slice(p * wid, wid, wid)]
+    v_bias = s.vec[1:2, wide_slice(p * wid, wid, wid)]
+    for k in range(4):
+        pp = plane_peers[k]
+        here = wide_slice(pp * chunk, chunk, chunk)
+        if k:
+            arrived(s.slow.at[pl.ds(0, chunk)], (N.slow, k))
+        low_chunk = s.slow[here, :]
+        krow = wide_slice(c * toks + pp * chunk, chunk, chunk)
+        s.kv[krow, 0:wid] = mm(low_chunk, s.wqkv[:, wid:2 * wid]).astype(BF16)
+        s.kv[krow, wid:2 * wid] = (mm(low_chunk, s.wqkv[:, 2 * wid:3 * wid]) + v_bias).astype(BF16)
+        remote(s.kv.at[krow], s.kv.at[krow], N.kv, N.kv, dev(other, z, p))
+        s.q[here, :] = (mm(low_chunk, s.wqkv[:, 0:wid]) + q_bias).astype(BF16)
+    kv_half = s.kv.at[wide_slice(c * toks, toks, toks)]
+    sent(kv_half, N.kv)
+
+    for k in (1, 2, 3):
+        arrived(s.wo.at[pl.ds(0, PLANES * rows)], (N.wop, k))
+    wo_half = s.wo.at[wide_slice(c * half, half, half)]
+    remote(wo_half, wo_half, N.wos, N.wos, dev(other, z, p))
+    sent(wo_half, N.wos)
+    arrived(kv_half, N.kv)
+
+    scale = HEAD ** (-0.5)
+    qt = TILE
+    s.att[...] = jnp.zeros_like(s.att)
+
+    def head_mask(h, n):
+        return lax.broadcasted_iota(jnp.int32, (n, wid), 1) // HEAD == h
+
+    def attend(step, carry):
+        h = step % heads
+        t = step // heads
+        here = wide_slice(t * qt, qt, qt)
+        mask = head_mask(h, qt)
+        queries = jnp.where(mask, s.q[here, :].astype(F32) * scale, 0.0).astype(BF16)
+        scores = mm(queries, s.kv[:, 0:wid], 1, 1) + s.bias[here, :]
+        top = jnp.max(scores, axis=-1, keepdims=True)
+        weights = jnp.exp(scores - top)
+        total = jnp.sum(weights, axis=-1, keepdims=True)
+        result = mm(weights.astype(BF16), s.kv[:, wid:2 * wid]) / total
+        s.att[here, :] = jnp.where(mask, result, s.att[here, :])
+        s.lse[h, here, :] = top + jnp.log(total)
+        return carry
+
+    lax.fori_loop(0, heads * (toks // qt), attend, 0)
+    s.attl[...] = s.att[...].astype(BF16)
+    for k in (1, 2, 3):
+        pp = plane_peers[k]
+        remote(
+            s.attl.at[wide_slice(pp * chunk, chunk, chunk)],
+            s.attx.at[:, wide_slice(p * wid, wid, wid)],
+            N.attx, (N.attx, k), dev(c, z, pp),
+        )
+    sent(s.attl.at[pl.ds(0, 3 * chunk)], N.attx)
+    s.attx[:, wide_slice(p * wid, wid, wid)] = s.attl[own_rows, :]
+
+    for k in (1, 2, 3):
+        arrived(s.win.at[pl.ds(0, zrows)], (N.wi2, k))
+        block = s.win.at[wide_slice(c * half + z_back[k] * zrows, zrows, zrows)]
+        remote(block, block, N.wi3, N.wi3, dev(other, z, p))
+    sent(s.win.at[pl.ds(0, half)], N.wi3)
+
+    arrived(s.wo.at[pl.ds(0, half)], N.wos)
+    for k in (1, 2, 3):
+        arrived(s.attl.at[pl.ds(0, chunk)], (N.attx, k))
+
+    def row_vec(r):
+        return s.vec[r:r + 1, :]
+
+    def normalize_rows(hidden_rows):
+        centered = hidden_rows - jnp.mean(hidden_rows, axis=-1, keepdims=True)
+        inverse = lax.rsqrt(jnp.mean(centered * centered, axis=-1, keepdims=True) + EPSILON)
+        return centered * inverse, inverse
+
+    branch = mm(s.attx[...], s.wo[...]) + row_vec(2)
+    normed, inverse = normalize_rows(s.sres[...] + branch)
+    s.n1[...] = normed
+    s.inv1[...] = inverse
+    after = normed * row_vec(3) + row_vec(4)
+    s.aft[...] = after
+    s.hid[own_rows, :] = after.astype(BF16)
+    plane_gather(s.hid, N.hid)
+
+    arrived(wfo_ref, N.wf0)
+    for k in (1, 2, 3):
+        arrived(s.wfo.at[pl.ds(0, frows)], (N.wf2, k))
+        block = s.wfo.at[wide_slice((c * 4 + z_back[k]) * frows, frows, frows)]
+        remote(block, block, N.wf3, N.wf3, dev(other, z, p))
+    sent(s.wfo.at[pl.ds(0, 4 * frows)], N.wf3)
+    arrived(s.win.at[pl.ds(0, half)], N.wi3)
+
+    def ffn_first(here):
+        def one(n, carry):
+            cols = wide_slice(n * TILE, TILE, TILE)
+            acc = mm(s.hid[here, :], s.win[:, cols]) + s.ffb[8:9, cols]
+            phi = 0.5 * (1.0 + lax.erf(acc * (2.0 ** -0.5)))
+            s.act[here, cols] = (acc * phi).astype(BF16)
+            s.pre[here, cols] = phi + acc * jnp.exp(-0.5 * acc * acc) * (1.0 / math.sqrt(2.0 * math.pi))
+            return carry
+        lax.fori_loop(0, units // TILE, one, 0)
+
+    def column_tiles(fn, total, dst, dst_rows=None):
+        def one(n, carry):
+            cols = wide_slice(n * TILE, TILE, TILE)
+            value = fn(cols).astype(dst.dtype)
+            if dst_rows is None:
+                dst[:, cols] = value
+            else:
+                dst[dst_rows, cols] = value
+            return carry
+        lax.fori_loop(0, total // TILE, one, 0)
+
+    def plane_scatter_step(k, fn, name):
+        if k:
+            column_tiles(fn, model, s.fs.at[k])
+            remote(s.fs.at[k], s.fr.at[k], name, (name, k), dev(c, z, plane_peers[k]))
+        else:
+            column_tiles(fn, model, s.own)
+
+    def plane_scatter_sum(name):
+        total = s.own[...]
+        for k in (1, 2, 3):
+            arrived(s.fr.at[k], (name, k))
+            total = total + s.fr[k].astype(F32)
+        return total
+
+    def plane_sent_now(name):
+        pltpu.make_async_copy(s.fs.at[pl.ds(0, 3)], s.fs.at[pl.ds(0, 3)], sem(SEND, name)).wait()
+
+    def chunk_rows(k):
+        return wide_slice(plane_peers[k] * chunk, chunk, chunk)
+
+    for k in range(4):
+        here = chunk_rows(k)
+        if k:
+            arrived(s.hid.at[pl.ds(0, chunk)], (N.hid, k))
+        ffn_first(here)
+        if k == 0:
+            arrived(s.wfo.at[pl.ds(0, 4 * frows)], N.wf3)
+        plane_scatter_step(k, lambda cols: mm(s.act[here, :], s.wfo[:, cols]), N.rs1)
+
+    branch = plane_scatter_sum(N.rs1) + row_vec(5)
+    normed2, inverse2 = normalize_rows(s.aft[...] + branch)
+    gain2 = row_vec(6)
+    s.outl[...] = (normed2 * gain2 + row_vec(7)).astype(BF16)
+    arrived(s.cin, N.c)
+    upstream = s.cin[...].astype(F32)
+    s.smg[...] = jnp.zeros_like(s.smg)
+    s.smg[6:7, :] = jnp.sum(upstream * normed2, axis=0, keepdims=True)
+    s.smg[7:8, :] = jnp.sum(upstream, axis=0, keepdims=True)
+
+    def norm_back(up, normed_rows, inverse_rows, gain):
+        scaled = up * gain
+        return inverse_rows * (
+            scaled
+            - jnp.mean(scaled, axis=-1, keepdims=True)
+            - normed_rows * jnp.mean(scaled * normed_rows, axis=-1, keepdims=True)
+        )
+
+    second = norm_back(upstream, normed2, inverse2, gain2)
+    s.second[...] = second
+    second_low = second.astype(BF16)
+    s.bg[own_rows, :] = second_low
+    plane_gather(s.bg, N.bg)
+    s.smg[5:6, :] = jnp.sum(second_low.astype(F32), axis=0, keepdims=True)
+
+    def send_home(src, dst, name):
+        for i in range(2):
+            is_self = jnp.logical_and(home == c, 2 * c + i == z)
+            maybe_local(
+                src.at[pl.ds(i * tok, tok)], dst.at[slot], (name, i), name,
+                dev(home, 2 * c + i, p), is_self,
+            )
+
+    send_home(s.outl, s.outr, N.out)
+
+    def ffn_back(here):
+        def one(n, carry):
+            cols = wide_slice(n * TILE, TILE, TILE)
+            acc = mm(s.bg[here, :], s.wfo[cols, :], 1, 1)
+            s.pg[here, cols] = (acc * s.pre[here, cols]).astype(BF16)
+            return carry
+        lax.fori_loop(0, units // TILE, one, 0)
+
+    plane_sent_now(N.rs1)
+    for k in range(4):
+        here = chunk_rows(k)
+        if k:
+            arrived(s.bg.at[pl.ds(0, chunk)], (N.bg, k))
+        ffn_back(here)
+        plane_scatter_step(k, lambda cols: mm(s.pg[here, :], s.win[cols, :], 1, 1), N.rs2)
+
+    def grad_sibling(lhs, rhs, buf_s, name):
+        def one(m, carry):
+            at = wide_slice(m * TILE, TILE, TILE)
+            cols = wide_slice(other * half + m * TILE, TILE, TILE)
+            buf_s[at, :] = mm(lhs[:, cols], rhs[...], 0, 0).astype(BF16)
+            return carry
+        lax.fori_loop(0, half // TILE, one, 0)
+
+    def sibling_send(buf_s, buf_r, name):
+        remote(buf_s, buf_r, name, name, dev(other, z, p))
+        sent(buf_s, name)
+
+    def grad_own(lhs, rhs, buf_r, buf_o, buf_zs, buf_zr, name):
+        arrived(buf_r, name)
+        for k in (1, 2, 3, 0):
+            at = wide_slice(z_peers[k] * zrows, zrows, zrows)
+            cols = wide_slice(c * half + z_peers[k] * zrows, zrows, zrows)
+            value = mm(lhs[:, cols], rhs[...], 0, 0) + buf_r[at, :].astype(F32)
+            if k:
+                buf_zs[k] = value.astype(BF16)
+                remote(buf_zs.at[k], buf_zr.at[k], (name, N.z), (name, N.z, k), dev(c, z_peers[k], p))
+            else:
+                buf_o[...] = value
+        sent(buf_zs.at[pl.ds(0, 3)], (name, N.z))
+
+    grad_sibling(s.act, s.bg, s.gfo_s, N.gfo)
+    sibling_send(s.gfo_s, s.gfo_r, N.gfo)
+    grad_sibling(s.hid, s.pg, s.gwi_s, N.gwi)
+    sibling_send(s.gwi_s, s.gwi_r, N.gwi)
+    s.smg[8:9, :] = jnp.sum(s.pg[...].astype(F32), axis=0, keepdims=True)
+
+    hidden_grad = s.second[...] + plane_scatter_sum(N.rs2)
+    normed = s.n1[...]
+    s.smg[3:4, :] = jnp.sum(hidden_grad * normed, axis=0, keepdims=True)
+    s.smg[4:5, :] = jnp.sum(hidden_grad, axis=0, keepdims=True)
+    first = norm_back(hidden_grad, normed, s.inv1[...], row_vec(3))
+    s.first[...] = first
+    first_low = first.astype(BF16)
+    s.agl[...] = first_low
+    s.smg[2:3, :] = jnp.sum(first_low.astype(F32), axis=0, keepdims=True)
+    column_tiles(lambda cols: mm(s.agl[...], s.wo[cols, :], 1, 1), model, s.ado)
+    for k in (1, 2, 3):
+        pp = plane_peers[k]
+        remote(
+            s.ado.at[:, wide_slice(pp * wid, wid, wid)],
+            s.do.at[own_rows],
+            N.do, (N.do, k), dev(c, z, pp),
+        )
+    sent(s.do.at[pl.ds(0, 3 * chunk)], N.do)
+    s.do[own_rows, :] = s.ado[:, wide_slice(p * wid, wid, wid)]
+
+    grad_own(s.act, s.bg, s.gfo_r, s.gfo_o, s.gfo_zs, s.gfo_zr, N.gfo)
+    grad_own(s.hid, s.pg, s.gwi_r, s.gwi_o, s.gwi_zs, s.gwi_zr, N.gwi)
+    grad_sibling(s.attx, s.agl, s.gwo_s, N.gwo)
+    sibling_send(s.gwo_s, s.gwo_r, N.gwo)
+
+    for k in (1, 2, 3):
+        arrived(s.do.at[pl.ds(0, chunk)], (N.do, k))
+
+    s.dq[...] = jnp.zeros_like(s.dq)
+    s.dk[...] = jnp.zeros_like(s.dk)
+    s.dv[...] = jnp.zeros_like(s.dv)
+
+    def attend_back(step, carry):
+        h = step % heads
+        t = step // heads
+        here = wide_slice(t * qt, qt, qt)
+        mask = head_mask(h, qt)
+        queries = jnp.where(mask, s.q[here, :].astype(F32) * scale, 0.0).astype(BF16)
+        scores = mm(queries, s.kv[:, 0:wid], 1, 1) + s.bias[here, :]
+        probs = jnp.exp(scores - s.lse[h, here, :])
+        grads = jnp.where(mask, s.do[here, :].astype(F32), 0.0)
+        residue = jnp.sum(grads * s.att[here, :], axis=-1, keepdims=True)
+        grads = grads.astype(BF16)
+        prob_grad = mm(grads, s.kv[:, wid:2 * wid], 1, 1)
+        score_grad = (probs * (prob_grad - residue)).astype(BF16)
+        s.dv[...] += mm(probs.astype(BF16), grads, 0, 0)
+        s.dk[...] += mm(score_grad, queries, 0, 0)
+        s.dq[here, :] += jnp.where(mask, mm(score_grad, s.kv[:, 0:wid]), 0.0)
+        return carry
+
+    lax.fori_loop(0, heads * (toks // qt), attend_back, 0)
+    theirs = wide_slice(other * toks, toks, toks)
+    mine = wide_slice(c * toks, toks, toks)
+    s.dkvs[:, 0:wid] = s.dk[theirs, :].astype(BF16)
+    s.dkvs[:, wid:2 * wid] = s.dv[theirs, :].astype(BF16)
+    sibling_send(s.dkvs, s.dkvr, N.dkv)
+    s.dqkv[:, 0:wid] = (s.dq[...] * scale).astype(BF16)
+
+    arrived(s.gwo_r, N.gwo)
+
+    def own_tile(m, carry):
+        at = wide_slice(m * TILE, TILE, TILE)
+        cols = wide_slice(c * half + m * TILE, TILE, TILE)
+        value = mm(s.attx[:, cols], s.agl[...], 0, 0) + s.gwo_r[at, :].astype(F32)
+        s.gwo_o[at, :] = value
+        s.gwo_p[at, :] = value.astype(BF16)
+        return carry
+
+    lax.fori_loop(0, half // TILE, own_tile, 0)
+
+    arrived(s.dkvr, N.dkv)
+    s.dqkv[:, wid:2 * wid] = (s.dk[mine, :] + s.dkvr[:, 0:wid].astype(F32)).astype(BF16)
+    s.dqkv[:, 2 * wid:3 * wid] = (s.dv[mine, :] + s.dkvr[:, wid:2 * wid].astype(F32)).astype(BF16)
+
+    plane_sent_now(N.rs2)
+    for k in (1, 2, 3, 0):
+        here = chunk_rows(k)
+        plane_scatter_step(k, lambda cols: mm(s.dqkv[here, :], s.wqkv[cols, :], 1, 1), N.rs3)
+
+    grad_sibling(s.slow, s.dqkv, s.gqk_s, N.gqk)
+    sibling_send(s.gqk_s, s.gqk_r, N.gqk)
+    for k in (1, 2, 3):
+        for zz in range(PLANES):
+            remote(
+                s.gwo_p.at[wide_slice(zz * zrows + plane_peers[k] * rows, rows, rows)],
+                s.gwo_pr.at[k, zz],
+                N.gwop, (N.gwop, k), dev(c, z, plane_peers[k]),
+            )
+    sent(s.gwo_p.at[pl.ds(0, 3 * PLANES * rows)], N.gwop)
+    grad_own(s.slow, s.dqkv, s.gqk_r, s.gqk_o, s.gqk_zs, s.gqk_zr, N.gqk)
+
+    low_sum = jnp.sum(s.dqkv[...].astype(F32), axis=0, keepdims=True)
+    pcols = wide_slice(p * wid, wid, wid)
+    s.smg[0:1, pcols] = low_sum[:, 0:wid]
+    s.smg[1:2, pcols] = low_sum[:, 2 * wid:3 * wid]
+    for cc in range(2):
+        for k in range(4):
+            if cc == 0 and k == 0:
+                continue
+            tc = other if cc else c
+            lanes = wide_slice((tc * 4 + z_peers[k]) * 128, 128, 128)
+            remote(s.smg.at[:, lanes], s.sma.at[cc * 4 + k], N.sma, (N.sma, cc, k), dev(tc, z_peers[k], p))
+    sent(s.smg.at[:, pl.ds(0, 7 * 128)], N.sma)
+
+    total = s.first[...] + plane_scatter_sum(N.rs3)
+    s.igl[...] = total.astype(BF16)
+    send_home(s.igl, s.igr, N.ig)
+
+    for k in (1, 2, 3):
+        arrived(s.gwo_pr.at[k], (N.gwop, k))
+
+    def gwo_total(zz):
+        value = s.gwo_o[wide_slice(zz * zrows + p * rows, rows, rows), :]
+        for k in (1, 2, 3):
+            value = value + s.gwo_pr[k, zz].astype(F32)
+        return value
+
+    for k in (1, 2, 3):
+        s.gwo_zs[k] = gwo_total(z_peers[k]).astype(BF16)
+        remote(s.gwo_zs.at[k], s.gwo_zr.at[k], N.gwoz, (N.gwoz, k), dev(c, z_peers[k], p))
+    sent(s.gwo_zs.at[pl.ds(0, 3)], N.gwoz)
+    dwo_ref[...] = gwo_total(z)
+
+    def z_total(buf_o, buf_zr, name):
+        total = buf_o[...]
+        for k in (1, 2, 3):
+            arrived(buf_zr.at[k], (name, N.z, k))
+            total = total + buf_zr[k].astype(F32)
+        return total
+
+    def plane_rows(buf_p, buf_pr, name):
+        for k in (1, 2, 3):
+            remote(
+                buf_p.at[wide_slice(plane_peers[k] * rows, rows, rows)], buf_pr.at[k],
+                name, (name, k), dev(c, z, plane_peers[k]),
+            )
+        sent(buf_p.at[pl.ds(0, 3 * rows)], name)
+
+    s.gwi_o[...] = z_total(s.gwi_o, s.gwi_zr, N.gwi)
+    s.gwi_p[...] = s.gwi_o[...].astype(BF16)
+    plane_rows(s.gwi_p, s.gwi_pr, N.gwip)
+    dwfo_ref[...] = z_total(s.gfo_o, s.gfo_zr, N.gfo)
+
+    part = s.smg[:, wide_slice((c * 4 + z) * 128, 128, 128)]
+    for cc in range(2):
+        for k in range(4):
+            if cc == 0 and k == 0:
+                continue
+            arrived(s.sma.at[cc * 4 + k], (N.sma, cc, k))
+            part = part + s.sma[cc * 4 + k]
+    s.smb[...] = part
+    for k in (1, 2, 3):
+        remote(s.smb, s.smb_r.at[k], N.smb, (N.smb, k), dev(c, z, plane_peers[k]))
+    sent(s.smb_r.at[pl.ds(0, 3)], N.smb)
+
+    s.gqk_o[...] = z_total(s.gqk_o, s.gqk_zr, N.gqk)
+    s.gqk_p[...] = s.gqk_o[...].astype(BF16)
+    plane_rows(s.gqk_p, s.gqk_pr, N.gqkp)
+
+    arrived(s.outr, N.out)
+    out_ref[...] = s.outr[...]
+
+    for k in range(4):
+        if k:
+            arrived(s.gwi_pr.at[k], (N.gwip, k))
+        pp = plane_peers[k]
+        for g in range(8):
+            piece_cols = slice(g * frows, (g + 1) * frows)
+            if k:
+                value = s.gwi_pr[k, :, piece_cols].astype(F32)
+            else:
+                value = s.gwi_o[wide_slice(p * rows, rows, rows), piece_cols]
+            dwin_ref[:, wide_slice(g * 4 * frows + pp * frows, frows, frows)] = value
+    for k in (1, 2, 3):
+        arrived(s.gwo_zr.at[k], (N.gwoz, k))
+        dwo_ref[...] += s.gwo_zr[k].astype(F32)
+    all_rows = s.smb[...]
+    for k in (1, 2, 3):
+        arrived(s.smb_r.at[k], (N.smb, k))
+        all_rows = all_rows + s.smb_r[k]
+    row_ids = lax.broadcasted_iota(jnp.int32, (16, 128), 0)
+    sg_ref[...] = jnp.where(row_ids == 8, s.smb[...], all_rows)
+    for k in range(4):
+        if k:
+            arrived(s.gqk_pr.at[k], (N.gqkp, k))
+        pp = plane_peers[k]
+        for t in range(3):
+            piece_cols = slice(t * wid, (t + 1) * wid)
+            if k:
+                value = s.gqk_pr[k, :, piece_cols].astype(F32)
+            else:
+                value = s.gqk_o[wide_slice(p * rows, rows, rows), piece_cols]
+            dwqkv_ref[:, wide_slice(t * model + pp * wid, wid, wid)] = value
+    arrived(s.igr, N.ig)
+    ig_ref[...] = s.igr[...]
+
+    @pl.when(table_here)
+    def _():
+        handle = sem(SEND, N.tbl)
+        pltpu.make_async_copy(s.tbl, s.tbl, handle).wait()
+
+    plane_sent_now(N.rs3)
+    flush_sent()
+
+
+def fused_local(
+    inputs, segments, pad_mask, timesteps, w_qkv, bias_query, bias_value, w_attn_out, bias_attn_out,
+    ln1_gain, ln1_shift, w_ffn_in, bias_ffn_in, w_ffn_out, bias_ffn_out, ln2_gain, ln2_shift, cotangent,
+):
+    _, tok, model = inputs.shape
+    hidden = w_ffn_in.shape[1]
+    rows = w_qkv.shape[0]
+    blk = lax.axis_index("blk")
+    half_width = model // 2
+    frequency = jnp.exp(
+        jnp.arange(half_width, dtype=F32) * (-math.log(10000.0) / half_width)
+    )
+    angles = timesteps.astype(F32)[..., None] * (100.0 / TSTEPS) * frequency
+    table = jnp.concatenate([jnp.sin(angles), jnp.cos(angles)], axis=-1)
+    vectors = jnp.stack(
+        [bias_query, bias_value, bias_attn_out, ln1_gain, ln1_shift, bias_ffn_out, ln2_gain, ln2_shift]
+    )
+    small = jnp.concatenate(
+        [
+            jnp.pad(vectors, ((0, 0), (0, 128 - rows))),
+            bias_ffn_in[None],
+            jnp.zeros((7, 128), BF16),
+        ]
+    )
+    codes = jnp.where(pad_mask == 1, segments, -1)
+    marks = jnp.stack([segments, codes], axis=1).astype(F32) + 1.0
+    odd = (blk // PLANE) % 2 == 1
+    marks = jnp.concatenate([jnp.where(odd, 0.0, marks), jnp.where(odd, marks, 0.0)], axis=-1)
+    info = jnp.pad(marks, ((0, 0), (0, 6), (0, 0)))
+
+    plan = scratch_plan(tok, model, hidden)
+    vmem = pl.BlockSpec(memory_space=pltpu.VMEM)
+    outs = pl.pallas_call(
+        functools.partial(fused, plan, tok, model, hidden),
+        out_shape=(
+            jax.ShapeDtypeStruct((2, tok, model), BF16),
+            jax.ShapeDtypeStruct((2, tok, model), BF16),
+            jax.ShapeDtypeStruct((rows, 3 * model), F32),
+            jax.ShapeDtypeStruct((rows, model), F32),
+            jax.ShapeDtypeStruct((rows, hidden), F32),
+            jax.ShapeDtypeStruct((hidden // 32, model), F32),
+            jax.ShapeDtypeStruct((16, 128), F32),
+        ),
+        in_specs=[vmem] * 9,
+        out_specs=[vmem] * 7,
+        scratch_shapes=[pltpu.VMEM(shape, dtype) for shape, dtype in plan.values()]
+        + [pltpu.SemaphoreType.DMA((N_SEND,)), pltpu.SemaphoreType.DMA((N_RECV,))],
+        compiler_params=pltpu.CompilerParams(
+            collective_id=0, has_side_effects=True, vmem_limit_bytes=63 * 1024 * 1024
+        ),
+    )(inputs, cotangent, table, small, info, w_qkv, w_attn_out, w_ffn_in, w_ffn_out)
+    out, input_grad, g_qkv, g_out, g_in, g_down, g_small = outs
+    mine = lax.dynamic_slice(g_small, (0, (blk % PLANE) * rows), (8, rows))
+    return (
+        out, input_grad, g_qkv, mine[0], mine[1], g_out, mine[2], mine[3], mine[4],
+        g_in, g_small[8], g_down, mine[5], mine[6], mine[7],
+    )
+
+
+def layer(*args):
+    inputs, w_qkv, w_ffn_out = args[0], args[4], args[13]
+    fits = (
+        lax.axis_size("dp") == 2
+        and lax.axis_size("blk") == PLANE * PLANES
+        and inputs.shape[0] == 2
+        and inputs.shape[1] == 64
+        and w_qkv.shape[0] * PLANE == 128
+        and w_ffn_out.shape[0] == 128
+        and args[3].shape[1] <= 8
+    )
+    return (fused_local if fits else local)(*args)
+
+
 def solution(mesh):
     return jax.shard_map(
-        local,
+        layer,
         mesh=mesh,
         in_specs=(
             P("dp", "blk", None),

time: 1680 us -> 226 us (0.13)
  waiting for transfers between devices: 1140 us -> 0 us
  blocking collectives: 317 us -> 0 us
  Pallas kernels: 0 us -> 209 us
  matrix products: 118 us -> 0 us
  local copies, waits for them, and re-layouts: 58.6 us -> 10.6 us
    reduce_scatter x4 -> x0, waiting for transfers between devices: 882 us -> none  [the longest x1 363 us: local(): lax.psum_scatter(down_weight_grad, ('dp', 'blk'), scatter_dimension=0, ti...]
    all_gather x8 -> x0, waiting for transfers between devices: 258 us -> none  [the longest x1 76.8 us: local(): lax.all_gather(w_ffn_in, ('dp', 'blk'), axis=0, tiled=True)]
    all_gather x5 -> x0, blocking collectives: 218 us -> none  [the longest x1 68.3 us: local(): lax.all_gather(bias_ffn_in, ('dp', 'blk'), axis=0, tiled=True)]
    pallas_call x0 -> x1, Pallas kernels: none -> 209 us  [fused_local(): pl.pallas_call(functools.partial(fused, plan, tok, model, hidden), out_sh...]
    dot_general x18 -> x0, matrix products: 118 us -> none  [the longest x1 11.3 us: local(): jnp.einsum('rqhk,rkhe->rqhe', score_grad, piece_keys, preferred_element_t...]
    unnamed x2 -> x0, blocking collectives: 99.3 us -> none
    all_gather x6 -> x0, local copies, waits for them, and re-layouts: 28.9 us -> none  [the longest x1 6.7 us: local(): lax.all_gather(value_send, 'blk', axis=1, tiled=True)]
  transfers between devices with their start and end apart: 12 -> 0, of which waited for: 8 -> 0; matrix products, arithmetic and copies ran while one was open for 11% -> 0% of each run, Pallas kernels for 0% -> 0%
where the time goes in v1:
time: 226 us; the launch traced here: 223 us
  Pallas kernels  209 us (92%)
  local copies, waits for them, and re-layouts  10.6 us (5%)
    pallas_call x1, Pallas kernels, fused_local(): pl.pallas_call(functools.partial(fused, plan, tok, model, hidden), out_sh...  209 us
    unnamed x42, local copies, waits for them, and re-layouts  9.39 us

profile of v1, /device:TPU:1, one launch (start us, length us, event | category | flops | bytes accessed | tf_op | source)
XLA Modules:
  0.0 223.1 jit_solution(2096633898396689645)
XLA Ops:
  0.7 0.1 pad.16.clone
  0.8 0.6 copy-done.7
  1.4 0.0 copy-done.5
  1.4 0.7 copy-done.8
  2.2 0.6 copy-done.10
  2.8 0.0 copy-done.11
  2.9 0.6 copy-done.9
  3.5 0.7 fusion.2.refs_3_
  4.2 0.7 select_maximum_fusion.refs_4_
  4.8 0.2 multiply_sine_fusion
  5.0 0.6 pad_maximum_fusion.refs_2_
  5.7 209.5 %shard_map.289 = (bf16[2,64,1024]{2,1,0:T(8,128)(2,1)}, bf16[2,64,1024]{2,1,0:T(8,128)(2,1)}, f32[32,3072]{1,0:T(8,128)}, f32[32,1024]{1,0:T(8,128)}, f32[32,409...) custom-call(bf16[2,64,1024]{2,1,0:T(8,128)(2,1)} %refs_0_.1, bf16[2,64,1024]{2,1,0:T(8,128)(2,1)} %refs_1_.1, ...), custom_call_target="tpu_custom_call" | custom-call | tf_op jit(solution)/shard_map/pallas_call | solution.py:1168
  215.2 0.7 copy-done.6
  215.9 0.5 slice_bitcast_fusion.3
  216.4 0.1 constant_dynamic-slice_fusion
  216.5 0.5 slice_bitcast_fusion
  217.0 1.7 copy.41
  218.7 0.7 copy.42
  219.5 0.7 copy.43
  220.2 0.2 copy-done.4
  220.4 0.7 copy.44
  221.1 0.8 copy.45
  221.9 0.4 copy-done
  222.3 0.8 copy.46
  (33 shorter events, 0.1 us)
Async XLA Ops:
  0.7 0.7 copy-start.7
  0.7 0.7 copy-start.5
  1.4 0.8 copy-start.15
  1.4 0.8 copy-start.16
  1.4 0.8 copy-start.17
  1.4 0.7 copy-start.8
  1.4 0.8 copy-start.14
  2.1 0.7 copy-start.10
  2.1 0.7 copy-start.11
  2.1 0.7 copy-start.12
  2.1 0.7 copy-start.13
  2.8 0.7 copy-start.9
  215.2 0.7 copy-start.6
  217.0 1.7 copy-start.3
  217.0 2.4 %copy-start.2 = (f32[32,3072]{1,0:T(8,128)S(1)}, f32[32,3072]{1,0:T(8,128)}, u32[]{:S(2)}) copy-start(f32[32,3072]{1,0:T(8,128)} %get-tuple-element.58) | copy-start | bytes 1179652
  219.4 1.0 copy-start.4
  219.5 1.7 copy-start.1
  221.1 1.2 copy-start

commit v2 on v1

--- a/solution.py
+++ b/solution.py
@@ -377,7 +377,7 @@
         pre=((toks, units), F32),
         act=((toks, units), BF16),
         fs=((PLANE, chunk, model), BF16),
-        fr=((PLANE, chunk, model), BF16),
+        fr=((3, chunk, model), BF16),
         own=((chunk, model), F32),
         outl=((chunk, model), BF16),
         outr=((2, tok, model), BF16),
@@ -400,19 +400,19 @@
         gfo_r=((half, model), BF16),
         gfo_o=((zrows, model), F32),
         gfo_zs=((4, zrows, model), BF16),
-        gfo_zr=((4, zrows, model), BF16),
+        gfo_zr=((5, zrows, model), BF16),
         gwi_s=((half, units), BF16),
         gwi_r=((half, units), BF16),
         gwi_o=((zrows, units), F32),
         gwi_zs=((4, zrows, units), BF16),
-        gwi_zr=((4, zrows, units), BF16),
+        gwi_zr=((5, zrows, units), BF16),
         gwi_p=((zrows, units), BF16),
         gwi_pr=((4, rows, units), BF16),
         gqk_s=((half, 3 * wid), BF16),
         gqk_r=((half, 3 * wid), BF16),
         gqk_o=((zrows, 3 * wid), F32),
         gqk_zs=((4, zrows, 3 * wid), BF16),
-        gqk_zr=((4, zrows, 3 * wid), BF16),
+        gqk_zr=((5, zrows, 3 * wid), BF16),
         gqk_p=((zrows, 3 * wid), BF16),
         gqk_pr=((4, rows, 3 * wid), BF16),
         gwo_s=((half, model), BF16),
@@ -420,8 +420,9 @@
         gwo_o=((half, model), F32),
         gwo_p=((half, model), BF16),
         gwo_pr=((4, PLANES, rows, model), BF16),
+        gwo_t=((rows, model), F32),
         gwo_zs=((4, rows, model), BF16),
-        gwo_zr=((4, rows, model), BF16),
+        gwo_zr=((5, rows, model), BF16),
         smg=((16, model), F32),
         sma=((8, 16, 128), F32),
         smb=((16, 128), F32),
@@ -429,7 +430,7 @@
     )
 
 
-N_SEND = 64
+N_SEND = 160
 N_RECV = 160
 
 
@@ -520,6 +521,172 @@
 
         sent(src, send_name, jnp.logical_not(is_self))
 
+    outer = z % 3 == 0
+    inner = jnp.logical_not(outer)
+    o_near, o_far, o_other = 1 + z // 3, 2 - z // 3, 3 - z
+    i_near, i_far, i_pair = 3 * (z - 1), 6 - 3 * z, 3 - z
+
+    class ZGather:
+        def __init__(self, name, block, half_ref, src=None, sibling=True):
+            self.name, self.block, self.src, self.sibling = name, block, src, sibling
+            one = block(0)
+            sent(one, (name, N.o), outer)
+            for key in (N.i0, N.f0, N.i1, N.f1, N.f2):
+                sent(one, (name, key), inner)
+            if sibling:
+                sent(half_ref, (name, N.s))
+            self.half_ref = half_ref
+
+        def send(self, zz, key, target, src=None):
+            ref = self.block(zz)
+            remote(ref if src is None else src, ref, (self.name, key), (self.name, key), dev(c, target, p))
+
+        def over(self, zz, src=None):
+            if self.sibling:
+                ref = self.block(zz)
+                remote(ref if src is None else src, ref, (self.name, N.s), (self.name, N.s), dev(other, z, p))
+
+        def take(self, zz, key):
+            arrived(self.block(zz), (self.name, key))
+
+        def step0(self):
+            @pl.when(outer)
+            def _():
+                self.send(z, N.o, o_near, self.src)
+
+            @pl.when(inner)
+            def _():
+                self.send(z, N.i0, i_pair, self.src)
+                self.send(z, N.f0, i_near, self.src)
+
+            self.over(z, self.src)
+
+        def step1(self):
+            @pl.when(inner)
+            def _():
+                self.take(i_near, N.o)
+                self.send(i_near, N.i1, i_pair)
+                self.take(i_pair, N.i0)
+                self.send(i_pair, N.f1, i_near)
+                self.over(i_near)
+                self.over(i_pair)
+
+            @pl.when(outer)
+            def _():
+                self.take(o_near, N.f0)
+                self.over(o_near)
+
+        def step2(self):
+            @pl.when(inner)
+            def _():
+                self.take(i_far, N.i1)
+                self.send(i_far, N.f2, i_near)
+                self.over(i_far)
+
+            @pl.when(outer)
+            def _():
+                self.take(o_far, N.f1)
+                self.over(o_far)
+
+        def step3(self):
+            @pl.when(outer)
+            def _():
+                self.take(o_other, N.f2)
+                self.over(o_other)
+
+        def done(self):
+            arrived(self.half_ref, (self.name, N.s))
+
+    class ZScatter:
+        def __init__(self, name, part, keep, got):
+            self.name, self.part, self.keep, self.got = name, part, keep, got
+            for key in (N.o0, N.o1, N.o2):
+                sent(part.at[0], (name, key), outer)
+            for key in (N.i0, N.i1, N.f):
+                sent(part.at[0], (name, key), inner)
+
+        def put(self, zz, value):
+            mine_block = zz == z
+
+            @pl.when(mine_block)
+            def _():
+                self.keep[...] = value
+
+            @pl.when(jnp.logical_not(mine_block))
+            def _():
+                self.part[zz] = value.astype(BF16)
+
+        def send(self, zz, slot_id, key, target):
+            remote(self.part.at[zz], self.got.at[slot_id], (self.name, key), (self.name, key), dev(c, target, p))
+
+        def take(self, slot_id, key):
+            arrived(self.got.at[slot_id], (self.name, key))
+            return self.got[slot_id].astype(F32)
+
+        def grow(self, zz, more):
+            self.part[zz] = (self.part[zz].astype(F32) + more).astype(BF16)
+
+        def step0(self):
+            @pl.when(outer)
+            def _():
+                self.send(o_other, 0, N.o0, o_near)
+                self.send(o_far, 1, N.o1, o_near)
+                self.send(o_near, 2, N.o2, o_near)
+
+        def step1(self):
+            @pl.when(inner)
+            def _():
+                self.grow(i_far, self.take(0, N.o0))
+                self.send(i_far, 3, N.i0, i_pair)
+                self.grow(i_pair, self.take(1, N.o1))
+                self.send(i_pair, 4, N.i1, i_pair)
+
+        def step2(self):
+            @pl.when(inner)
+            def _():
+                self.grow(i_near, self.take(3, N.i0))
+                self.send(i_near, 0, N.f, i_near)
+                self.keep[...] += self.take(2, N.o2)
+
+        def step3(self):
+            @pl.when(inner)
+            def _():
+                self.keep[...] += self.take(4, N.i1)
+
+            @pl.when(outer)
+            def _():
+                self.keep[...] += self.take(0, N.f)
+
+    class PlaneGather:
+        def __init__(self, name, pieces, sizes):
+            self.name, self.pieces, self.sizes = name, pieces, sizes
+            for k in (1, 2):
+                for h in (0, 1):
+                    sent(sizes[h], (name, k, h))
+                sent(sizes[2 - k], (name, 3, k))
+
+        def send(self, pp, h, target, key, recv_key):
+            for ref in self.pieces(pp, h):
+                remote(ref, ref, (self.name,) + key, (self.name,) + recv_key, dev(c, z, target))
+
+        def step0(self):
+            for h in (1, 0):
+                self.send(p, h, plane_peers[2], (2, h), (2, h))
+                self.send(p, 1 - h, plane_peers[1], (1, 1 - h), (1, 1 - h))
+
+        def step1(self):
+            arrived(self.sizes[0], (self.name, 1, 0))
+            self.send(plane_peers[1], 0, plane_peers[2], (3, 2), (3, 0))
+            arrived(self.sizes[1], (self.name, 2, 1))
+            self.send(plane_peers[2], 1, plane_peers[1], (3, 1), (3, 1))
+
+        def done(self, k):
+            if k in (1, 2):
+                arrived(self.sizes[2 - k], (self.name, k, 2 - k))
+            if k == 3:
+                for h in (0, 1):
+                    arrived(self.sizes[h], (self.name, 3, h))
+
     barrier = pltpu.get_barrier_semaphore()
     greeted = [dev(c, z, plane_peers[k]) for k in (1, 2, 3)]
     greeted += [dev(c, z_peers[k], p) for k in (1, 2, 3)]
@@ -543,6 +710,11 @@
     def _():
         remote(table_ref.at[slot], s.tbl, N.tbl, N.tbl, dev(other, z, p))
         s.tbl[...] = table_ref[slot]
+
+    s.smalls[c, z, p] = small_ref[...]
+    for k in (1, 2, 3):
+        remote(small_ref, s.smalls.at[c, z, p], N.smz, (N.smz, k), dev(c, z_peers[k], p))
+    sent(s.smalls.at[0, 0, pl.ds(0, 3)], N.smz)
 
     wrow = (c * 16 + z * 4 + p) * rows
     for t in range(3):
@@ -561,64 +733,21 @@
             )
         sent(s.wqkv.at[pl.ds(0, rows)], (N.wq1, k))
 
-    s.smalls[c, z, p] = small_ref[...]
-    for k in (1, 2, 3):
-        remote(small_ref, s.smalls.at[c, z, p], N.smz, (N.smz, k), dev(c, z_peers[k], p))
-    sent(s.smalls.at[0, 0, pl.ds(0, 3)], N.smz)
-
-    pltpu.make_async_copy(wo_ref, s.wo.at[wide_slice(wrow, rows, rows)], sem(RECV, N.wo0)).start()
-    for k in (1, 2, 3):
-        remote(wo_ref, s.wo.at[wide_slice(wrow, rows, rows)], N.woz, (N.woz, k), dev(c, z_peers[k], p))
-    sent(s.wo.at[pl.ds(0, 3 * rows)], N.woz)
-
+    wo_block = s.wo.at[wide_slice(wrow, rows, rows)]
+    pltpu.make_async_copy(wo_ref, wo_block, sem(RECV, N.wo0)).start()
+    woz = ZGather(
+        N.woz, lambda zz: s.wo.at[wide_slice((c * 16 + zz * 4 + p) * rows, rows, rows)], None, src=wo_ref, sibling=False
+    )
+    woz.step0()
     arrived(s.wqkv.at[pl.ds(0, rows)], N.wq0)
     for k in (1, 2, 3):
         arrived(s.wqkv.at[pl.ds(0, rows)], (N.wq1, k))
     zrow = c * half + z * zrows
-    wq_block = s.wqkv.at[wide_slice(zrow, zrows, zrows)]
-    for k in (1, 2, 3):
-        remote(wq_block, wq_block, N.wq2, (N.wq2, k), dev(c, z_peers[k], p))
-    sent(s.wqkv.at[pl.ds(0, 3 * zrows)], N.wq2)
-    remote(wq_block, wq_block, N.wq3, N.wq3, dev(other, z, p))
-
-    arrived(s.inf_in, N.i)
-    info_own = s.inf_in[0] + s.inf_in[1]
-    s.inf[c * 4 + p] = info_own
-    for k in (1, 2, 3):
-        blk_ref = s.inf.at[c * 4 + p]
-        remote(blk_ref, blk_ref, N.inf, (N.inf, k), dev(c, z, plane_peers[k]))
-    sent(s.inf.at[pl.ds(0, 3)], N.inf)
-
-    @pl.when(jnp.logical_not(table_here))
-    def _():
-        arrived(s.tbl, N.tbl)
-
-    arrived(s.xin, N.x)
-    items = lax.broadcasted_iota(jnp.int32, (8, chunk), 0).astype(F32)
-    onehot = jnp.where(info_own[0:1, :] == items + 1.0, 1.0, 0.0)
-    embedded = lax.dot_general(
-        onehot, s.tbl[...], (((0,), (0,)), ((), ())), precision=lax.Precision.HIGHEST,
-        preferred_element_type=F32,
-    )
-    start_res = s.xin[...].astype(F32) + embedded
-    s.sres[...] = start_res
-    prow = p * chunk
-    own_rows = wide_slice(prow, chunk, chunk)
-    s.slow[own_rows, :] = start_res.astype(BF16)
-
-    def plane_gather(ref, name):
-        for k in (1, 2, 3):
-            block = ref.at[own_rows]
-            remote(block, block, name, (name, k), dev(c, z, plane_peers[k]))
-        sent(ref.at[pl.ds(0, 3 * chunk)], name)
-
-    plane_gather(s.slow, N.slow)
-
-    for i in range(2):
-        plane_of = 2 * c + i
-        is_self = jnp.logical_and(home == c, plane_of == z)
-        target = dev(home, plane_of, p)
-        maybe_local(cot_ref.at[i], s.cin.at[wide_slice(slot * tok, tok, tok)], (N.c, i), N.c, target, is_self)
+    wq = ZGather(
+        N.wq, lambda zz: s.wqkv.at[wide_slice(c * half + zz * zrows, zrows, zrows)], s.wqkv.at[pl.ds(0, half)]
+    )
+    wq.step0()
+
     for g in range(8):
         pltpu.make_async_copy(
             win_ref.at[:, wide_slice(g * 4 * frows + p * frows, frows, frows)],
@@ -634,6 +763,42 @@
                 (N.wi1, k), (N.wi1, k), dev(c, z, pp),
             )
         sent(s.win.at[pl.ds(0, rows)], (N.wi1, k))
+    arrived(s.inf_in, N.i)
+    info_own = s.inf_in[0] + s.inf_in[1]
+    s.inf[c * 4 + p] = info_own
+    for k in (1, 2, 3):
+        blk_ref = s.inf.at[c * 4 + p]
+        remote(blk_ref, blk_ref, N.inf, (N.inf, k), dev(c, z, plane_peers[k]))
+    sent(s.inf.at[pl.ds(0, 3)], N.inf)
+
+    @pl.when(jnp.logical_not(table_here))
+    def _():
+        arrived(s.tbl, N.tbl)
+
+    arrived(s.xin, N.x)
+    items = lax.broadcasted_iota(jnp.int32, (8, chunk), 0).astype(F32)
+    onehot = jnp.where(info_own[0:1, :] == items + 1.0, 1.0, 0.0)
+    embedded = lax.dot_general(
+        onehot, s.tbl[...], (((0,), (0,)), ((), ())), precision=lax.Precision.HIGHEST,
+        preferred_element_type=F32,
+    )
+    start_res = s.xin[...].astype(F32) + embedded
+    s.sres[...] = start_res
+    prow = p * chunk
+    own_rows = wide_slice(prow, chunk, chunk)
+    s.slow[own_rows, :] = start_res.astype(BF16)
+
+    def plane_gather(ref, name):
+        gather = PlaneGather(
+            name,
+            lambda pp, h: [ref.at[wide_slice(pp * chunk + h * tok, tok, tok)]],
+            (ref.at[pl.ds(0, tok)], ref.at[pl.ds(0, tok)]),
+        )
+        gather.step0()
+        return gather
+
+    slow_gather = plane_gather(s.slow, N.slow)
+
     for k in (1, 2, 3):
         arrived(s.smalls.at[0, 0, 0], (N.smz, k))
     for k in (1, 2, 3):
@@ -641,34 +806,32 @@
             ref = s.smalls.at[c, zz, p]
             remote(ref, ref, N.smp, (N.smp, k), dev(c, z, plane_peers[k]))
     sent(s.smalls.at[0, pl.ds(0, 3)], N.smp)
+    wq.step1()
+    woz.step1()
     for k in (1, 2, 3):
         arrived(s.inf.at[0], (N.inf, k))
     inf_half = s.inf.at[wide_slice(c * 4, 4, 4)]
     remote(inf_half, inf_half, N.infs, N.infs, dev(other, z, p))
     sent(inf_half, N.infs)
+    slow_gather.step1()
+    arrived(s.win.at[pl.ds(0, rows)], N.wi0)
+    for k in (1, 2, 3):
+        arrived(s.win.at[pl.ds(0, rows)], (N.wi1, k))
+    wi = ZGather(
+        N.wi, lambda zz: s.win.at[wide_slice(c * half + zz * zrows, zrows, zrows)], s.win.at[pl.ds(0, half)]
+    )
+    fblock = (c * 4 + z) * frows
+    pltpu.make_async_copy(wfo_ref, s.wfo.at[wide_slice(fblock, frows, frows)], sem(RECV, N.wf0)).start()
+    wf = ZGather(
+        N.wf, lambda zz: s.wfo.at[wide_slice((c * 4 + zz) * frows, frows, frows)], s.wfo.at[pl.ds(0, 4 * frows)], src=wfo_ref
+    )
+    wq.step2()
+    woz.step2()
+    wi.step0()
     for k in (1, 2, 3):
         arrived(s.smalls.at[0, 0], (N.smp, k))
     remote(s.smalls.at[c], s.smalls.at[c], N.sms, N.sms, dev(other, z, p))
     sent(s.smalls.at[0], N.sms)
-    arrived(wo_ref, N.wo0)
-    for k in (1, 2, 3):
-        arrived(wo_ref, (N.woz, k))
-    arrived(s.win.at[pl.ds(0, rows)], N.wi0)
-    for k in (1, 2, 3):
-        arrived(s.win.at[pl.ds(0, rows)], (N.wi1, k))
-    wi_block = s.win.at[wide_slice(zrow, zrows, zrows)]
-    for k in (1, 2, 3):
-        remote(wi_block, wi_block, N.wi2, (N.wi2, k), dev(c, z_peers[k], p))
-    sent(s.win.at[pl.ds(0, 3 * zrows)], N.wi2)
-    remote(wi_block, wi_block, N.wi3, N.wi3, dev(other, z, p))
-    fblock = (c * 4 + z) * frows
-    f_ref = s.wfo.at[wide_slice(fblock, frows, frows)]
-    pltpu.make_async_copy(wfo_ref, f_ref, sem(RECV, N.wf0)).start()
-    for k in (1, 2, 3):
-        remote(wfo_ref, f_ref, N.wf2, (N.wf2, k), dev(c, z_peers[k], p))
-    sent(s.wfo.at[pl.ds(0, 3 * frows)], N.wf2)
-    remote(wfo_ref, f_ref, N.wf3, N.wf3, dev(other, z, p))
-
     arrived(s.smalls.at[0], N.sms)
     pieces = s.smalls[...].reshape(512, 128)
     lane = lax.broadcasted_iota(jnp.int32, (128, model), 1)
@@ -692,25 +855,15 @@
     seg_hot = jnp.concatenate(seg_hot, axis=1)
     s.bias[...] = (mm(seg_hot, code_hot, 0, 0) - 1.0) * -NEGATIVE
 
-    for k in (1, 2, 3):
-        arrived(s.wqkv.at[pl.ds(0, zrows)], (N.wq2, k))
-        block = s.wqkv.at[wide_slice(c * half + z_back[k] * zrows, zrows, zrows)]
-        remote(block, block, N.wq3, N.wq3, dev(other, z, p))
-    sent(s.wqkv.at[pl.ds(0, half)], N.wq3)
-    for zz in range(PLANES):
-        block = s.wo.at[wide_slice((c * 16 + zz * 4 + p) * rows, rows, rows)]
-        for k in (1, 2, 3):
-            remote(block, block, N.wop, (N.wop, k), dev(c, z, plane_peers[k]))
-    sent(s.wo.at[pl.ds(0, 3 * PLANES * rows)], N.wop)
-    arrived(s.wqkv.at[pl.ds(0, half)], N.wq3)
+    wq.step3()
+    wq.done()
 
     q_bias = s.vec[0:1, wide_slice(p * wid, wid, wid)]
     v_bias = s.vec[1:2, wide_slice(p * wid, wid, wid)]
     for k in range(4):
         pp = plane_peers[k]
         here = wide_slice(pp * chunk, chunk, chunk)
-        if k:
-            arrived(s.slow.at[pl.ds(0, chunk)], (N.slow, k))
+        slow_gather.done(k)
         low_chunk = s.slow[here, :]
         krow = wide_slice(c * toks + pp * chunk, chunk, chunk)
         s.kv[krow, 0:wid] = mm(low_chunk, s.wqkv[:, wid:2 * wid]).astype(BF16)
@@ -720,11 +873,18 @@
     kv_half = s.kv.at[wide_slice(c * toks, toks, toks)]
     sent(kv_half, N.kv)
 
-    for k in (1, 2, 3):
-        arrived(s.wo.at[pl.ds(0, PLANES * rows)], (N.wop, k))
-    wo_half = s.wo.at[wide_slice(c * half, half, half)]
-    remote(wo_half, wo_half, N.wos, N.wos, dev(other, z, p))
-    sent(wo_half, N.wos)
+    woz.step3()
+    arrived(wo_ref, N.wo0)
+    wop = PlaneGather(
+        N.wop,
+        lambda pp, h: [
+            s.wo.at[wide_slice((c * 16 + (2 * h + g) * 4 + pp) * rows, rows, rows)] for g in range(2)
+        ],
+        (s.wo.at[pl.ds(0, 2 * rows)], s.wo.at[pl.ds(0, 2 * rows)]),
+    )
+    wop.step0()
+    wi.step1()
+    wf.step0()
     arrived(kv_half, N.kv)
 
     scale = HEAD ** (-0.5)
@@ -749,7 +909,11 @@
         s.lse[h, here, :] = top + jnp.log(total)
         return carry
 
-    lax.fori_loop(0, heads * (toks // qt), attend, 0)
+    steps = heads * (toks // qt)
+    lax.fori_loop(0, steps // 2, attend, 0)
+    wop.step1()
+    wf.step1()
+    lax.fori_loop(steps // 2, steps, attend, 0)
     s.attl[...] = s.att[...].astype(BF16)
     for k in (1, 2, 3):
         pp = plane_peers[k]
@@ -761,12 +925,12 @@
     sent(s.attl.at[pl.ds(0, 3 * chunk)], N.attx)
     s.attx[:, wide_slice(p * wid, wid, wid)] = s.attl[own_rows, :]
 
-    for k in (1, 2, 3):
-        arrived(s.win.at[pl.ds(0, zrows)], (N.wi2, k))
-        block = s.win.at[wide_slice(c * half + z_back[k] * zrows, zrows, zrows)]
-        remote(block, block, N.wi3, N.wi3, dev(other, z, p))
-    sent(s.win.at[pl.ds(0, half)], N.wi3)
-
+    wi.step2()
+    for k in (1, 2, 3):
+        wop.done(k)
+    wo_half = s.wo.at[wide_slice(c * half, half, half)]
+    remote(wo_half, wo_half, N.wos, N.wos, dev(other, z, p))
+    sent(wo_half, N.wos)
     arrived(s.wo.at[pl.ds(0, half)], N.wos)
     for k in (1, 2, 3):
         arrived(s.attl.at[pl.ds(0, chunk)], (N.attx, k))
@@ -786,15 +950,16 @@
     after = normed * row_vec(3) + row_vec(4)
     s.aft[...] = after
     s.hid[own_rows, :] = after.astype(BF16)
-    plane_gather(s.hid, N.hid)
-
+    hid_gather = plane_gather(s.hid, N.hid)
+
+    for i in range(2):
+        plane_of = 2 * c + i
+        is_self = jnp.logical_and(home == c, plane_of == z)
+        target = dev(home, plane_of, p)
+        maybe_local(cot_ref.at[i], s.cin.at[wide_slice(slot * tok, tok, tok)], (N.c, i), N.c, target, is_self)
     arrived(wfo_ref, N.wf0)
-    for k in (1, 2, 3):
-        arrived(s.wfo.at[pl.ds(0, frows)], (N.wf2, k))
-        block = s.wfo.at[wide_slice((c * 4 + z_back[k]) * frows, frows, frows)]
-        remote(block, block, N.wf3, N.wf3, dev(other, z, p))
-    sent(s.wfo.at[pl.ds(0, 4 * frows)], N.wf3)
-    arrived(s.win.at[pl.ds(0, half)], N.wi3)
+    wi.step3()
+    wi.done()
 
     def ffn_first(here):
         def one(n, carry):
@@ -817,34 +982,65 @@
             return carry
         lax.fori_loop(0, total // TILE, one, 0)
 
-    def plane_scatter_step(k, fn, name):
-        if k:
-            column_tiles(fn, model, s.fs.at[k])
-            remote(s.fs.at[k], s.fr.at[k], name, (name, k), dev(c, z, plane_peers[k]))
-        else:
+    top_half, low_half = pl.ds(0, tok), pl.ds(tok, tok)
+    rs_keys = ((1, 0), (1, 1), (2, 0), (2, 1), (3, 0), (3, 1))
+
+    def scatter_send(name, k, h, dst, target):
+        rows_of = (top_half, low_half)[h]
+        remote(s.fs.at[k, rows_of], dst.at[rows_of], (name, k, h), (name, k, h), dev(c, z, plane_peers[target]))
+
+    def plane_scatter_chunk(k, fn, name):
+        if k == 0:
             column_tiles(fn, model, s.own)
+            return
+        column_tiles(fn, model, s.fs.at[k])
+        scatter_start(k, name)
+
+    def scatter_start(k, name):
+        if k == 1:
+            scatter_send(name, 1, 0, s.fr.at[1], 1)
+        if k == 2:
+            scatter_send(name, 2, 1, s.fr.at[2], 2)
+        if k == 3:
+            scatter_send(name, 3, 0, s.fr.at[0], 1)
+            scatter_send(name, 3, 1, s.fr.at[0], 2)
+
+    def plane_scatter_pass(name):
+        for h, k in ((0, 2), (1, 1)):
+            rows_of = (top_half, low_half)[h]
+            arrived(s.fr.at[0, rows_of], (name, 3, h))
+            s.fs[k, rows_of, :] = (
+                s.fs[k, rows_of, :].astype(F32) + s.fr[0, rows_of, :].astype(F32)
+            ).astype(BF16)
+            scatter_send(name, k, h, s.fr.at[k], k)
 
     def plane_scatter_sum(name):
-        total = s.own[...]
-        for k in (1, 2, 3):
-            arrived(s.fr.at[k], (name, k))
-            total = total + s.fr[k].astype(F32)
-        return total
+        for k in (1, 2):
+            for h in (0, 1):
+                arrived(s.fr.at[k, top_half], (name, k, h))
+        return s.own[...] + s.fr[1].astype(F32) + s.fr[2].astype(F32)
 
     def plane_sent_now(name):
-        pltpu.make_async_copy(s.fs.at[pl.ds(0, 3)], s.fs.at[pl.ds(0, 3)], sem(SEND, name)).wait()
+        for k, h in rs_keys:
+            ref = s.fs.at[k, top_half]
+            pltpu.make_async_copy(ref, ref, sem(SEND, (name, k, h))).wait()
 
     def chunk_rows(k):
         return wide_slice(plane_peers[k] * chunk, chunk, chunk)
 
     for k in range(4):
         here = chunk_rows(k)
-        if k:
-            arrived(s.hid.at[pl.ds(0, chunk)], (N.hid, k))
+        hid_gather.done(k)
         ffn_first(here)
         if k == 0:
-            arrived(s.wfo.at[pl.ds(0, 4 * frows)], N.wf3)
-        plane_scatter_step(k, lambda cols: mm(s.act[here, :], s.wfo[:, cols]), N.rs1)
+            hid_gather.step1()
+            wf.step2()
+    wf.step3()
+    wf.done()
+    for k in (3, 1, 2, 0):
+        here = chunk_rows(k)
+        plane_scatter_chunk(k, lambda cols: mm(s.act[here, :], s.wfo[:, cols]), N.rs1)
+    plane_scatter_pass(N.rs1)
 
     branch = plane_scatter_sum(N.rs1) + row_vec(5)
     normed2, inverse2 = normalize_rows(s.aft[...] + branch)
@@ -868,7 +1064,7 @@
     s.second[...] = second
     second_low = second.astype(BF16)
     s.bg[own_rows, :] = second_low
-    plane_gather(s.bg, N.bg)
+    bg_gather = plane_gather(s.bg, N.bg)
     s.smg[5:6, :] = jnp.sum(second_low.astype(F32), axis=0, keepdims=True)
 
     def send_home(src, dst, name):
@@ -889,14 +1085,6 @@
             return carry
         lax.fori_loop(0, units // TILE, one, 0)
 
-    plane_sent_now(N.rs1)
-    for k in range(4):
-        here = chunk_rows(k)
-        if k:
-            arrived(s.bg.at[pl.ds(0, chunk)], (N.bg, k))
-        ffn_back(here)
-        plane_scatter_step(k, lambda cols: mm(s.pg[here, :], s.win[cols, :], 1, 1), N.rs2)
-
     def grad_sibling(lhs, rhs, buf_s, name):
         def one(m, carry):
             at = wide_slice(m * TILE, TILE, TILE)
@@ -909,24 +1097,46 @@
         remote(buf_s, buf_r, name, name, dev(other, z, p))
         sent(buf_s, name)
 
-    def grad_own(lhs, rhs, buf_r, buf_o, buf_zs, buf_zr, name):
+    def grad_own(lhs, rhs, buf_r, scatter, name):
         arrived(buf_r, name)
-        for k in (1, 2, 3, 0):
+        for k in (2, 3, 1, 0):
             at = wide_slice(z_peers[k] * zrows, zrows, zrows)
             cols = wide_slice(c * half + z_peers[k] * zrows, zrows, zrows)
             value = mm(lhs[:, cols], rhs[...], 0, 0) + buf_r[at, :].astype(F32)
             if k:
-                buf_zs[k] = value.astype(BF16)
-                remote(buf_zs.at[k], buf_zr.at[k], (name, N.z), (name, N.z, k), dev(c, z_peers[k], p))
+                scatter.part[z_peers[k]] = value.astype(BF16)
             else:
-                buf_o[...] = value
-        sent(buf_zs.at[pl.ds(0, 3)], (name, N.z))
-
-    grad_sibling(s.act, s.bg, s.gfo_s, N.gfo)
-    sibling_send(s.gfo_s, s.gfo_r, N.gfo)
+                scatter.keep[...] = value
+        scatter.step0()
+
+    gfo = ZScatter((N.gfo, N.z), s.gfo_zs, s.gfo_o, s.gfo_zr)
+    gwi = ZScatter((N.gwi, N.z), s.gwi_zs, s.gwi_o, s.gwi_zr)
+    gqk = ZScatter((N.gqk, N.z), s.gqk_zs, s.gqk_o, s.gqk_zr)
+    gwo = ZScatter((N.gwo, N.z), s.gwo_zs, s.gwo_t, s.gwo_zr)
+
+    plane_sent_now(N.rs1)
+
+    def hidden_chunk(k):
+        here = chunk_rows(k)
+        plane_scatter_chunk(k, lambda cols: mm(s.pg[here, :], s.win[cols, :], 1, 1), N.rs2)
+
+    for k in range(4):
+        bg_gather.done(k)
+        if k == 3:
+            grad_sibling(s.act, s.bg, s.gfo_s, N.gfo)
+            sibling_send(s.gfo_s, s.gfo_r, N.gfo)
+        ffn_back(chunk_rows(k))
+        if k == 0:
+            bg_gather.step1()
+        else:
+            hidden_chunk(k)
+    grad_own(s.act, s.bg, s.gfo_r, gfo, N.gfo)
+    plane_scatter_pass(N.rs2)
     grad_sibling(s.hid, s.pg, s.gwi_s, N.gwi)
     sibling_send(s.gwi_s, s.gwi_r, N.gwi)
+    hidden_chunk(0)
     s.smg[8:9, :] = jnp.sum(s.pg[...].astype(F32), axis=0, keepdims=True)
+    grad_own(s.hid, s.pg, s.gwi_r, gwi, N.gwi)
 
     hidden_grad = s.second[...] + plane_scatter_sum(N.rs2)
     normed = s.n1[...]
@@ -948,8 +1158,6 @@
     sent(s.do.at[pl.ds(0, 3 * chunk)], N.do)
     s.do[own_rows, :] = s.ado[:, wide_slice(p * wid, wid, wid)]
 
-    grad_own(s.act, s.bg, s.gfo_r, s.gfo_o, s.gfo_zs, s.gfo_zr, N.gfo)
-    grad_own(s.hid, s.pg, s.gwi_r, s.gwi_o, s.gwi_zs, s.gwi_zr, N.gwi)
     grad_sibling(s.attx, s.agl, s.gwo_s, N.gwo)
     sibling_send(s.gwo_s, s.gwo_r, N.gwo)
 
@@ -978,14 +1186,7 @@
         s.dq[here, :] += jnp.where(mask, mm(score_grad, s.kv[:, 0:wid]), 0.0)
         return carry
 
-    lax.fori_loop(0, heads * (toks // qt), attend_back, 0)
-    theirs = wide_slice(other * toks, toks, toks)
-    mine = wide_slice(c * toks, toks, toks)
-    s.dkvs[:, 0:wid] = s.dk[theirs, :].astype(BF16)
-    s.dkvs[:, wid:2 * wid] = s.dv[theirs, :].astype(BF16)
-    sibling_send(s.dkvs, s.dkvr, N.dkv)
-    s.dqkv[:, 0:wid] = (s.dq[...] * scale).astype(BF16)
-
+    lax.fori_loop(0, steps // 4, attend_back, 0)
     arrived(s.gwo_r, N.gwo)
 
     def own_tile(m, carry):
@@ -998,17 +1199,6 @@
 
     lax.fori_loop(0, half // TILE, own_tile, 0)
 
-    arrived(s.dkvr, N.dkv)
-    s.dqkv[:, wid:2 * wid] = (s.dk[mine, :] + s.dkvr[:, 0:wid].astype(F32)).astype(BF16)
-    s.dqkv[:, 2 * wid:3 * wid] = (s.dv[mine, :] + s.dkvr[:, wid:2 * wid].astype(F32)).astype(BF16)
-
-    plane_sent_now(N.rs2)
-    for k in (1, 2, 3, 0):
-        here = chunk_rows(k)
-        plane_scatter_step(k, lambda cols: mm(s.dqkv[here, :], s.wqkv[cols, :], 1, 1), N.rs3)
-
-    grad_sibling(s.slow, s.dqkv, s.gqk_s, N.gqk)
-    sibling_send(s.gqk_s, s.gqk_r, N.gqk)
     for k in (1, 2, 3):
         for zz in range(PLANES):
             remote(
@@ -1017,7 +1207,31 @@
                 N.gwop, (N.gwop, k), dev(c, z, plane_peers[k]),
             )
     sent(s.gwo_p.at[pl.ds(0, 3 * PLANES * rows)], N.gwop)
-    grad_own(s.slow, s.dqkv, s.gqk_r, s.gqk_o, s.gqk_zs, s.gqk_zr, N.gqk)
+    gfo.step1()
+    lax.fori_loop(steps // 4, steps, attend_back, 0)
+    gfo.step2()
+    theirs = wide_slice(other * toks, toks, toks)
+    mine = wide_slice(c * toks, toks, toks)
+    s.dkvs[:, 0:wid] = s.dk[theirs, :].astype(BF16)
+    s.dkvs[:, wid:2 * wid] = s.dv[theirs, :].astype(BF16)
+    sibling_send(s.dkvs, s.dkvr, N.dkv)
+    s.dqkv[:, 0:wid] = (s.dq[...] * scale).astype(BF16)
+
+    arrived(s.dkvr, N.dkv)
+    s.dqkv[:, wid:2 * wid] = (s.dk[mine, :] + s.dkvr[:, 0:wid].astype(F32)).astype(BF16)
+    s.dqkv[:, 2 * wid:3 * wid] = (s.dv[mine, :] + s.dkvr[:, wid:2 * wid].astype(F32)).astype(BF16)
+
+    plane_sent_now(N.rs2)
+    for k in (3, 1, 2, 0):
+        here = chunk_rows(k)
+        plane_scatter_chunk(k, lambda cols: mm(s.dqkv[here, :], s.wqkv[cols, :], 1, 1), N.rs3)
+
+    grad_sibling(s.slow, s.dqkv, s.gqk_s, N.gqk)
+    sibling_send(s.gqk_s, s.gqk_r, N.gqk)
+    plane_scatter_pass(N.rs3)
+    gwi.step1()
+    grad_own(s.slow, s.dqkv, s.gqk_r, gqk, N.gqk)
+    gwi.step2()
 
     low_sum = jnp.sum(s.dqkv[...].astype(F32), axis=0, keepdims=True)
     pcols = wide_slice(p * wid, wid, wid)
@@ -1045,18 +1259,12 @@
             value = value + s.gwo_pr[k, zz].astype(F32)
         return value
 
-    for k in (1, 2, 3):
-        s.gwo_zs[k] = gwo_total(z_peers[k]).astype(BF16)
-        remote(s.gwo_zs.at[k], s.gwo_zr.at[k], N.gwoz, (N.gwoz, k), dev(c, z_peers[k], p))
-    sent(s.gwo_zs.at[pl.ds(0, 3)], N.gwoz)
-    dwo_ref[...] = gwo_total(z)
-
-    def z_total(buf_o, buf_zr, name):
-        total = buf_o[...]
-        for k in (1, 2, 3):
-            arrived(buf_zr.at[k], (name, N.z, k))
-            total = total + buf_zr[k].astype(F32)
-        return total
+    for k in (2, 3, 1):
+        s.gwo_zs[z_peers[k]] = gwo_total(z_peers[k]).astype(BF16)
+    s.gwo_t[...] = gwo_total(z)
+    gwo.step0()
+
+    gwi.step3()
 
     def plane_rows(buf_p, buf_pr, name):
         for k in (1, 2, 3):
@@ -1066,31 +1274,14 @@
             )
         sent(buf_p.at[pl.ds(0, 3 * rows)], name)
 
-    s.gwi_o[...] = z_total(s.gwi_o, s.gwi_zr, N.gwi)
     s.gwi_p[...] = s.gwi_o[...].astype(BF16)
     plane_rows(s.gwi_p, s.gwi_pr, N.gwip)
-    dwfo_ref[...] = z_total(s.gfo_o, s.gfo_zr, N.gfo)
-
-    part = s.smg[:, wide_slice((c * 4 + z) * 128, 128, 128)]
-    for cc in range(2):
-        for k in range(4):
-            if cc == 0 and k == 0:
-                continue
-            arrived(s.sma.at[cc * 4 + k], (N.sma, cc, k))
-            part = part + s.sma[cc * 4 + k]
-    s.smb[...] = part
-    for k in (1, 2, 3):
-        remote(s.smb, s.smb_r.at[k], N.smb, (N.smb, k), dev(c, z, plane_peers[k]))
-    sent(s.smb_r.at[pl.ds(0, 3)], N.smb)
-
-    s.gqk_o[...] = z_total(s.gqk_o, s.gqk_zr, N.gqk)
-    s.gqk_p[...] = s.gqk_o[...].astype(BF16)
-    plane_rows(s.gqk_p, s.gqk_pr, N.gqkp)
-
-    arrived(s.outr, N.out)
-    out_ref[...] = s.outr[...]
-
-    for k in range(4):
+    gfo.step3()
+    dwfo_ref[...] = s.gfo_o[...]
+    gqk.step1()
+    gwo.step1()
+
+    def dwin_piece(k):
         if k:
             arrived(s.gwi_pr.at[k], (N.gwip, k))
         pp = plane_peers[k]
@@ -1101,9 +1292,31 @@
             else:
                 value = s.gwi_o[wide_slice(p * rows, rows, rows), piece_cols]
             dwin_ref[:, wide_slice(g * 4 * frows + pp * frows, frows, frows)] = value
-    for k in (1, 2, 3):
-        arrived(s.gwo_zr.at[k], (N.gwoz, k))
-        dwo_ref[...] += s.gwo_zr[k].astype(F32)
+
+    part = s.smg[:, wide_slice((c * 4 + z) * 128, 128, 128)]
+    for cc in range(2):
+        for k in range(4):
+            if cc == 0 and k == 0:
+                continue
+            arrived(s.sma.at[cc * 4 + k], (N.sma, cc, k))
+            part = part + s.sma[cc * 4 + k]
+    s.smb[...] = part
+    for k in (1, 2, 3):
+        remote(s.smb, s.smb_r.at[k], N.smb, (N.smb, k), dev(c, z, plane_peers[k]))
+    sent(s.smb_r.at[pl.ds(0, 3)], N.smb)
+
+    gqk.step2()
+    gwo.step2()
+    arrived(s.outr, N.out)
+    out_ref[...] = s.outr[...]
+    for k in range(4):
+        dwin_piece(k)
+    gqk.step3()
+    s.gqk_p[...] = s.gqk_o[...].astype(BF16)
+    plane_rows(s.gqk_p, s.gqk_pr, N.gqkp)
+
+    gwo.step3()
+    dwo_ref[...] = s.gwo_t[...]
     all_rows = s.smb[...]
     for k in (1, 2, 3):
         arrived(s.smb_r.at[k], (N.smb, k))

time: 226 us -> 189 us (0.84); the launches traced: 223 us -> 188 us
  Pallas kernels: 209 us -> 175 us
    pallas_call x1, Pallas kernels: 209 us -> 175 us  [fused_local(): pl.pallas_call(functools.partial(fused, plan, tok, model, hidden), out_sh...]
where the time goes in v2:
time: 189 us; the launch traced here: 188 us
  Pallas kernels  175 us (93%)
  local copies, waits for them, and re-layouts  10.6 us (6%)
  other arithmetic  2.2 us (1%)
    pallas_call x1, Pallas kernels, fused_local(): pl.pallas_call(functools.partial(fused, plan, tok, model, hidden), out_sh...  175 us
    unnamed x42, local copies, waits for them, and re-layouts  9.39 us

profile of v2, /device:TPU:1, one launch (start us, length us, event | category | flops | bytes accessed | tf_op | source)
XLA Modules:
  0.0 188.4 jit_solution(2320522325092915312)
XLA Ops:
  0.7 0.1 pad.16.clone
  0.8 0.6 copy-done.7
  1.4 0.0 copy-done.5
  1.4 0.7 copy-done.8
  2.2 0.6 copy-done.10
  2.8 0.0 copy-done.11
  2.9 0.6 copy-done.9
  3.5 0.7 fusion.2.refs_3_
  4.2 0.7 select_maximum_fusion.refs_4_
  4.8 0.2 multiply_sine_fusion
  5.0 0.6 pad_maximum_fusion.refs_2_
  5.7 174.8 %shard_map.289 = (bf16[2,64,1024]{2,1,0:T(8,128)(2,1)}, bf16[2,64,1024]{2,1,0:T(8,128)(2,1)}, f32[32,3072]{1,0:T(8,128)}, f32[32,1024]{1,0:T(8,128)}, f32[32,409...) custom-call(bf16[2,64,1024]{2,1,0:T(8,128)(2,1)} %refs_0_.1, bf16[2,64,1024]{2,1,0:T(8,128)(2,1)} %refs_1_.1, ...), custom_call_target="tpu_custom_call" | custom-call | tf_op jit(solution)/shard_map/pallas_call | solution.py:1381
  180.5 0.7 copy-done.6
  181.2 0.5 slice_bitcast_fusion.3
  181.7 0.1 constant_dynamic-slice_fusion
  181.8 0.5 slice_bitcast_fusion
  182.3 1.7 copy.41
  184.1 0.7 copy.42
  184.8 0.7 copy.43
  185.5 0.2 copy-done.4
  185.8 0.7 copy.44
  186.4 0.8 copy.45
  187.2 0.4 copy-done
  187.6 0.8 copy.46
  (33 shorter events, 0.1 us)
Async XLA Ops:
  0.7 0.7 copy-start.7
  0.7 0.7 copy-start.5
  1.4 0.8 copy-start.15
  1.4 0.8 copy-start.16
  1.4 0.8 copy-start.17
  1.4 0.7 copy-start.8
  1.4 0.8 copy-start.14
  2.1 0.7 copy-start.10
  2.1 0.7 copy-start.11
  2.1 0.7 copy-start.12
  2.1 0.7 copy-start.13
  2.8 0.7 copy-start.9
  180.5 0.7 copy-start.6
  182.3 1.7 copy-start.3
  182.3 2.4 %copy-start.2 = (f32[32,3072]{1,0:T(8,128)S(1)}, f32[32,3072]{1,0:T(8,128)}, u32[]{:S(2)}) copy-start(f32[32,3072]{1,0:T(8,128)} %get-tuple-element.58) | copy-start | bytes 1179652
  184.8 1.0 copy-start.4
  184.8 1.7 copy-start.1
  186.4 1.2 copy-start

commit v3 on v2

--- a/solution.py
+++ b/solution.py
@@ -424,6 +424,8 @@
         gwo_zs=((4, rows, model), BF16),
         gwo_zr=((5, rows, model), BF16),
         smg=((16, model), F32),
+        stq=((PLANE, rows, 3 * wid), BF16),
+        sti=((PLANE, rows, units), BF16),
         sma=((8, 16, 128), F32),
         smb=((16, 128), F32),
         smb_r=((4, 16, 128), F32),
@@ -626,12 +628,17 @@
         def grow(self, zz, more):
             self.part[zz] = (self.part[zz].astype(F32) + more).astype(BF16)
 
-        def step0(self):
+        def start(self, j):
+            if j == 3:
+                return
+
             @pl.when(outer)
             def _():
-                self.send(o_other, 0, N.o0, o_near)
-                self.send(o_far, 1, N.o1, o_near)
-                self.send(o_near, 2, N.o2, o_near)
+                self.send((o_other, o_far, o_near)[j], j, (N.o0, N.o1, N.o2)[j], o_near)
+
+        def step0(self):
+            for j in range(3):
+                self.start(j)
 
         def step1(self):
             @pl.when(inner)
@@ -693,6 +700,20 @@
     greeted += [dev(other, z_peers[k], p) for k in (0, 1, 2, 3)]
     for target in greeted:
         pl.semaphore_signal(barrier, inc=1, device_id=target, device_id_type=MESH)
+    wrow = (c * 16 + z * 4 + p) * rows
+    own_w = wide_slice(wrow, rows, rows)
+    fblock = (c * 4 + z) * frows
+    for pp in range(PLANE):
+        for t in range(3):
+            s.stq[pp, :, t * wid:(t + 1) * wid] = wqkv_ref[:, t * model + pp * wid:t * model + (pp + 1) * wid]
+        for g in range(8):
+            source = (g * PLANE + pp) * frows
+            s.sti[pp, :, g * frows:(g + 1) * frows] = win_ref[:, source:source + frows]
+    s.wqkv[own_w, :] = s.stq[p]
+    s.win[own_w, :] = s.sti[p]
+    s.wo[own_w, :] = wo_ref[...]
+    s.wfo[wide_slice(fblock, frows, frows), :] = wfo_ref[...]
+    s.smalls[c, z, p] = small_ref[...]
     pl.semaphore_wait(barrier, len(greeted))
 
     home = z // 2
@@ -711,58 +732,35 @@
         remote(table_ref.at[slot], s.tbl, N.tbl, N.tbl, dev(other, z, p))
         s.tbl[...] = table_ref[slot]
 
-    s.smalls[c, z, p] = small_ref[...]
+    for k in (3, 1, 2):
+        pp = plane_peers[k]
+        remote(s.stq.at[pp], s.wqkv.at[own_w], (N.wq1, k), (N.wq1, k), dev(c, z, pp))
+        sent(s.stq.at[0], (N.wq1, k))
+    woz = ZGather(
+        N.woz, lambda zz: s.wo.at[wide_slice((c * 16 + zz * 4 + p) * rows, rows, rows)], None, src=wo_ref, sibling=False
+    )
+    wf = ZGather(
+        N.wf, lambda zz: s.wfo.at[wide_slice((c * 4 + zz) * frows, frows, frows)], s.wfo.at[pl.ds(0, 4 * frows)], src=wfo_ref
+    )
     for k in (1, 2, 3):
         remote(small_ref, s.smalls.at[c, z, p], N.smz, (N.smz, k), dev(c, z_peers[k], p))
     sent(s.smalls.at[0, 0, pl.ds(0, 3)], N.smz)
 
-    wrow = (c * 16 + z * 4 + p) * rows
-    for t in range(3):
-        pltpu.make_async_copy(
-            wqkv_ref.at[:, wide_slice(t * model + p * wid, wid, wid)],
-            s.wqkv.at[wide_slice(wrow, rows, rows), pl.ds(t * wid, wid)],
-            sem(RECV, N.wq0),
-        ).start()
+    wi = ZGather(
+        N.wi, lambda zz: s.win.at[wide_slice(c * half + zz * zrows, zrows, zrows)], s.win.at[pl.ds(0, half)]
+    )
+    woz.step0()
     for k in (3, 1, 2):
         pp = plane_peers[k]
-        for t in range(3):
-            remote(
-                wqkv_ref.at[:, wide_slice(t * model + pp * wid, wid, wid)],
-                s.wqkv.at[wide_slice(wrow, rows, rows), pl.ds(t * wid, wid)],
-                (N.wq1, k), (N.wq1, k), dev(c, z, pp),
-            )
-        sent(s.wqkv.at[pl.ds(0, rows)], (N.wq1, k))
-
-    wo_block = s.wo.at[wide_slice(wrow, rows, rows)]
-    pltpu.make_async_copy(wo_ref, wo_block, sem(RECV, N.wo0)).start()
-    woz = ZGather(
-        N.woz, lambda zz: s.wo.at[wide_slice((c * 16 + zz * 4 + p) * rows, rows, rows)], None, src=wo_ref, sibling=False
-    )
-    woz.step0()
-    arrived(s.wqkv.at[pl.ds(0, rows)], N.wq0)
-    for k in (1, 2, 3):
-        arrived(s.wqkv.at[pl.ds(0, rows)], (N.wq1, k))
-    zrow = c * half + z * zrows
+        remote(s.sti.at[pp], s.win.at[own_w], (N.wi1, k), (N.wi1, k), dev(c, z, pp))
+        sent(s.sti.at[0], (N.wi1, k))
+    for k in (1, 2, 3):
+        arrived(s.stq.at[0], (N.wq1, k))
     wq = ZGather(
         N.wq, lambda zz: s.wqkv.at[wide_slice(c * half + zz * zrows, zrows, zrows)], s.wqkv.at[pl.ds(0, half)]
     )
     wq.step0()
 
-    for g in range(8):
-        pltpu.make_async_copy(
-            win_ref.at[:, wide_slice(g * 4 * frows + p * frows, frows, frows)],
-            s.win.at[wide_slice(wrow, rows, rows), pl.ds(g * frows, frows)],
-            sem(RECV, N.wi0),
-        ).start()
-    for k in (3, 1, 2):
-        pp = plane_peers[k]
-        for g in range(8):
-            remote(
-                win_ref.at[:, wide_slice(g * 4 * frows + pp * frows, frows, frows)],
-                s.win.at[wide_slice(wrow, rows, rows), pl.ds(g * frows, frows)],
-                (N.wi1, k), (N.wi1, k), dev(c, z, pp),
-            )
-        sent(s.win.at[pl.ds(0, rows)], (N.wi1, k))
     arrived(s.inf_in, N.i)
     info_own = s.inf_in[0] + s.inf_in[1]
     s.inf[c * 4 + p] = info_own
@@ -806,32 +804,24 @@
             ref = s.smalls.at[c, zz, p]
             remote(ref, ref, N.smp, (N.smp, k), dev(c, z, plane_peers[k]))
     sent(s.smalls.at[0, pl.ds(0, 3)], N.smp)
-    wq.step1()
-    woz.step1()
     for k in (1, 2, 3):
         arrived(s.inf.at[0], (N.inf, k))
     inf_half = s.inf.at[wide_slice(c * 4, 4, 4)]
     remote(inf_half, inf_half, N.infs, N.infs, dev(other, z, p))
     sent(inf_half, N.infs)
+    for k in (1, 2, 3):
+        arrived(s.sti.at[0], (N.wi1, k))
+    wi.step0()
     slow_gather.step1()
-    arrived(s.win.at[pl.ds(0, rows)], N.wi0)
-    for k in (1, 2, 3):
-        arrived(s.win.at[pl.ds(0, rows)], (N.wi1, k))
-    wi = ZGather(
-        N.wi, lambda zz: s.win.at[wide_slice(c * half + zz * zrows, zrows, zrows)], s.win.at[pl.ds(0, half)]
-    )
-    fblock = (c * 4 + z) * frows
-    pltpu.make_async_copy(wfo_ref, s.wfo.at[wide_slice(fblock, frows, frows)], sem(RECV, N.wf0)).start()
-    wf = ZGather(
-        N.wf, lambda zz: s.wfo.at[wide_slice((c * 4 + zz) * frows, frows, frows)], s.wfo.at[pl.ds(0, 4 * frows)], src=wfo_ref
-    )
-    wq.step2()
-    woz.step2()
-    wi.step0()
+    wq.step1()
+    woz.step1()
     for k in (1, 2, 3):
         arrived(s.smalls.at[0, 0], (N.smp, k))
     remote(s.smalls.at[c], s.smalls.at[c], N.sms, N.sms, dev(other, z, p))
     sent(s.smalls.at[0], N.sms)
+    wf.step0()
+    wq.step2()
+    woz.step2()
     arrived(s.smalls.at[0], N.sms)
     pieces = s.smalls[...].reshape(512, 128)
     lane = lax.broadcasted_iota(jnp.int32, (128, model), 1)
@@ -874,7 +864,6 @@
     sent(kv_half, N.kv)
 
     woz.step3()
-    arrived(wo_ref, N.wo0)
     wop = PlaneGather(
         N.wop,
         lambda pp, h: [
@@ -884,7 +873,6 @@
     )
     wop.step0()
     wi.step1()
-    wf.step0()
     arrived(kv_half, N.kv)
 
     scale = HEAD ** (-0.5)
@@ -910,9 +898,10 @@
         return carry
 
     steps = heads * (toks // qt)
-    lax.fori_loop(0, steps // 2, attend, 0)
+    lax.fori_loop(0, steps // 4, attend, 0)
+    wf.step1()
+    lax.fori_loop(steps // 4, steps // 2, attend, 0)
     wop.step1()
-    wf.step1()
     lax.fori_loop(steps // 2, steps, attend, 0)
     s.attl[...] = s.att[...].astype(BF16)
     for k in (1, 2, 3):
@@ -925,7 +914,6 @@
     sent(s.attl.at[pl.ds(0, 3 * chunk)], N.attx)
     s.attx[:, wide_slice(p * wid, wid, wid)] = s.attl[own_rows, :]
 
-    wi.step2()
     for k in (1, 2, 3):
         wop.done(k)
     wo_half = s.wo.at[wide_slice(c * half, half, half)]
@@ -945,19 +933,20 @@
 
     branch = mm(s.attx[...], s.wo[...]) + row_vec(2)
     normed, inverse = normalize_rows(s.sres[...] + branch)
+    after = normed * row_vec(3) + row_vec(4)
+    s.hid[own_rows, :] = after.astype(BF16)
+    hid_gather = plane_gather(s.hid, N.hid)
     s.n1[...] = normed
     s.inv1[...] = inverse
-    after = normed * row_vec(3) + row_vec(4)
     s.aft[...] = after
-    s.hid[own_rows, :] = after.astype(BF16)
-    hid_gather = plane_gather(s.hid, N.hid)
-
+    wi.step2()
+    wf.step2()
     for i in range(2):
         plane_of = 2 * c + i
         is_self = jnp.logical_and(home == c, plane_of == z)
         target = dev(home, plane_of, p)
         maybe_local(cot_ref.at[i], s.cin.at[wide_slice(slot * tok, tok, tok)], (N.c, i), N.c, target, is_self)
-    arrived(wfo_ref, N.wf0)
+
     wi.step3()
     wi.done()
 
@@ -969,7 +958,7 @@
             s.act[here, cols] = (acc * phi).astype(BF16)
             s.pre[here, cols] = phi + acc * jnp.exp(-0.5 * acc * acc) * (1.0 / math.sqrt(2.0 * math.pi))
             return carry
-        lax.fori_loop(0, units // TILE, one, 0)
+        lax.fori_loop(0, units // TILE, one, 0, unroll=True)
 
     def column_tiles(fn, total, dst, dst_rows=None):
         def one(n, carry):
@@ -980,7 +969,7 @@
             else:
                 dst[dst_rows, cols] = value
             return carry
-        lax.fori_loop(0, total // TILE, one, 0)
+        lax.fori_loop(0, total // TILE, one, 0, unroll=True)
 
     top_half, low_half = pl.ds(0, tok), pl.ds(tok, tok)
     rs_keys = ((1, 0), (1, 1), (2, 0), (2, 1), (3, 0), (3, 1))
@@ -1034,7 +1023,6 @@
         ffn_first(here)
         if k == 0:
             hid_gather.step1()
-            wf.step2()
     wf.step3()
     wf.done()
     for k in (3, 1, 2, 0):
@@ -1045,12 +1033,8 @@
     branch = plane_scatter_sum(N.rs1) + row_vec(5)
     normed2, inverse2 = normalize_rows(s.aft[...] + branch)
     gain2 = row_vec(6)
-    s.outl[...] = (normed2 * gain2 + row_vec(7)).astype(BF16)
     arrived(s.cin, N.c)
     upstream = s.cin[...].astype(F32)
-    s.smg[...] = jnp.zeros_like(s.smg)
-    s.smg[6:7, :] = jnp.sum(upstream * normed2, axis=0, keepdims=True)
-    s.smg[7:8, :] = jnp.sum(upstream, axis=0, keepdims=True)
 
     def norm_back(up, normed_rows, inverse_rows, gain):
         scaled = up * gain
@@ -1061,10 +1045,14 @@
         )
 
     second = norm_back(upstream, normed2, inverse2, gain2)
-    s.second[...] = second
     second_low = second.astype(BF16)
     s.bg[own_rows, :] = second_low
     bg_gather = plane_gather(s.bg, N.bg)
+    s.second[...] = second
+    s.outl[...] = (normed2 * gain2 + row_vec(7)).astype(BF16)
+    s.smg[...] = jnp.zeros_like(s.smg)
+    s.smg[6:7, :] = jnp.sum(upstream * normed2, axis=0, keepdims=True)
+    s.smg[7:8, :] = jnp.sum(upstream, axis=0, keepdims=True)
     s.smg[5:6, :] = jnp.sum(second_low.astype(F32), axis=0, keepdims=True)
 
     def send_home(src, dst, name):
@@ -1083,31 +1071,30 @@
             acc = mm(s.bg[here, :], s.wfo[cols, :], 1, 1)
             s.pg[here, cols] = (acc * s.pre[here, cols]).astype(BF16)
             return carry
-        lax.fori_loop(0, units // TILE, one, 0)
-
-    def grad_sibling(lhs, rhs, buf_s, name):
-        def one(m, carry):
-            at = wide_slice(m * TILE, TILE, TILE)
-            cols = wide_slice(other * half + m * TILE, TILE, TILE)
+        lax.fori_loop(0, units // TILE, one, 0, unroll=True)
+
+    def turn(j):
+        return (z // 2) * (2 * j - 3) + 3 - j
+
+    def grad_sibling(lhs, rhs, buf_s, buf_r, name):
+        for j in range(4):
+            at = wide_slice(turn(j) * zrows, zrows, zrows)
+            cols = wide_slice(other * half + turn(j) * zrows, zrows, zrows)
             buf_s[at, :] = mm(lhs[:, cols], rhs[...], 0, 0).astype(BF16)
-            return carry
-        lax.fori_loop(0, half // TILE, one, 0)
+            remote(buf_s.at[at], buf_r.at[at], (name, j), (name, j), dev(other, z, p))
+            sent(buf_s.at[pl.ds(0, zrows)], (name, j))
 
     def sibling_send(buf_s, buf_r, name):
         remote(buf_s, buf_r, name, name, dev(other, z, p))
         sent(buf_s, name)
 
     def grad_own(lhs, rhs, buf_r, scatter, name):
-        arrived(buf_r, name)
-        for k in (2, 3, 1, 0):
-            at = wide_slice(z_peers[k] * zrows, zrows, zrows)
-            cols = wide_slice(c * half + z_peers[k] * zrows, zrows, zrows)
-            value = mm(lhs[:, cols], rhs[...], 0, 0) + buf_r[at, :].astype(F32)
-            if k:
-                scatter.part[z_peers[k]] = value.astype(BF16)
-            else:
-                scatter.keep[...] = value
-        scatter.step0()
+        for j in range(4):
+            at = wide_slice(turn(j) * zrows, zrows, zrows)
+            cols = wide_slice(c * half + turn(j) * zrows, zrows, zrows)
+            arrived(buf_r.at[pl.ds(0, zrows)], (name, j))
+            scatter.put(turn(j), mm(lhs[:, cols], rhs[...], 0, 0) + buf_r[at, :].astype(F32))
+            scatter.start(j)
 
     gfo = ZScatter((N.gfo, N.z), s.gfo_zs, s.gfo_o, s.gfo_zr)
     gwi = ZScatter((N.gwi, N.z), s.gwi_zs, s.gwi_o, s.gwi_zr)
@@ -1123,43 +1110,39 @@
     for k in range(4):
         bg_gather.done(k)
         if k == 3:
-            grad_sibling(s.act, s.bg, s.gfo_s, N.gfo)
-            sibling_send(s.gfo_s, s.gfo_r, N.gfo)
+            grad_sibling(s.act, s.bg, s.gfo_s, s.gfo_r, N.gfo)
         ffn_back(chunk_rows(k))
+        if k == 3:
+            grad_own(s.act, s.bg, s.gfo_r, gfo, N.gfo)
         if k == 0:
             bg_gather.step1()
         else:
             hidden_chunk(k)
-    grad_own(s.act, s.bg, s.gfo_r, gfo, N.gfo)
     plane_scatter_pass(N.rs2)
-    grad_sibling(s.hid, s.pg, s.gwi_s, N.gwi)
-    sibling_send(s.gwi_s, s.gwi_r, N.gwi)
+    grad_sibling(s.hid, s.pg, s.gwi_s, s.gwi_r, N.gwi)
     hidden_chunk(0)
     s.smg[8:9, :] = jnp.sum(s.pg[...].astype(F32), axis=0, keepdims=True)
     grad_own(s.hid, s.pg, s.gwi_r, gwi, N.gwi)
 
     hidden_grad = s.second[...] + plane_scatter_sum(N.rs2)
     normed = s.n1[...]
+    first = norm_back(hidden_grad, normed, s.inv1[...], row_vec(3))
+    first_low = first.astype(BF16)
+    s.agl[...] = first_low
+    for k in (3, 1, 2, 0):
+        pp = plane_peers[k]
+        cols = wide_slice(pp * wid, wid, wid)
+        s.ado[:, cols] = mm(first_low, s.wo[cols, :], 1, 1).astype(BF16)
+        if k:
+            remote(s.ado.at[:, cols], s.do.at[own_rows], N.do, (N.do, k), dev(c, z, pp))
+    sent(s.do.at[pl.ds(0, 3 * chunk)], N.do)
+    s.first[...] = first
     s.smg[3:4, :] = jnp.sum(hidden_grad * normed, axis=0, keepdims=True)
     s.smg[4:5, :] = jnp.sum(hidden_grad, axis=0, keepdims=True)
-    first = norm_back(hidden_grad, normed, s.inv1[...], row_vec(3))
-    s.first[...] = first
-    first_low = first.astype(BF16)
-    s.agl[...] = first_low
     s.smg[2:3, :] = jnp.sum(first_low.astype(F32), axis=0, keepdims=True)
-    column_tiles(lambda cols: mm(s.agl[...], s.wo[cols, :], 1, 1), model, s.ado)
-    for k in (1, 2, 3):
-        pp = plane_peers[k]
-        remote(
-            s.ado.at[:, wide_slice(pp * wid, wid, wid)],
-            s.do.at[own_rows],
-            N.do, (N.do, k), dev(c, z, pp),
-        )
-    sent(s.do.at[pl.ds(0, 3 * chunk)], N.do)
     s.do[own_rows, :] = s.ado[:, wide_slice(p * wid, wid, wid)]
 
-    grad_sibling(s.attx, s.agl, s.gwo_s, N.gwo)
-    sibling_send(s.gwo_s, s.gwo_r, N.gwo)
+    grad_sibling(s.attx, s.agl, s.gwo_s, s.gwo_r, N.gwo)
 
     for k in (1, 2, 3):
         arrived(s.do.at[pl.ds(0, chunk)], (N.do, k))
@@ -1187,7 +1170,8 @@
         return carry
 
     lax.fori_loop(0, steps // 4, attend_back, 0)
-    arrived(s.gwo_r, N.gwo)
+    for j in range(4):
+        arrived(s.gwo_r.at[pl.ds(0, zrows)], (N.gwo, j))
 
     def own_tile(m, carry):
         at = wide_slice(m * TILE, TILE, TILE)
@@ -1208,8 +1192,11 @@
             )
     sent(s.gwo_p.at[pl.ds(0, 3 * PLANES * rows)], N.gwop)
     gfo.step1()
-    lax.fori_loop(steps // 4, steps, attend_back, 0)
+    lax.fori_loop(steps // 4, steps // 2, attend_back, 0)
+    lax.fori_loop(steps // 2, 3 * steps // 4, attend_back, 0)
     gfo.step2()
+    lax.fori_loop(3 * steps // 4, steps, attend_back, 0)
+    gwi.step1()
     theirs = wide_slice(other * toks, toks, toks)
     mine = wide_slice(c * toks, toks, toks)
     s.dkvs[:, 0:wid] = s.dk[theirs, :].astype(BF16)
@@ -1217,6 +1204,20 @@
     sibling_send(s.dkvs, s.dkvr, N.dkv)
     s.dqkv[:, 0:wid] = (s.dq[...] * scale).astype(BF16)
 
+    for k in (1, 2, 3):
+        arrived(s.gwo_pr.at[k], (N.gwop, k))
+
+    def gwo_total(zz):
+        value = s.gwo_o[wide_slice(zz * zrows + p * rows, rows, rows), :]
+        for k in (1, 2, 3):
+            value = value + s.gwo_pr[k, zz].astype(F32)
+        return value
+
+    for k in (2, 3, 1):
+        s.gwo_zs[z_peers[k]] = gwo_total(z_peers[k]).astype(BF16)
+    s.gwo_t[...] = gwo_total(z)
+    gwo.step0()
+
     arrived(s.dkvr, N.dkv)
     s.dqkv[:, wid:2 * wid] = (s.dk[mine, :] + s.dkvr[:, 0:wid].astype(F32)).astype(BF16)
     s.dqkv[:, 2 * wid:3 * wid] = (s.dv[mine, :] + s.dkvr[:, wid:2 * wid].astype(F32)).astype(BF16)
@@ -1226,12 +1227,11 @@
         here = chunk_rows(k)
         plane_scatter_chunk(k, lambda cols: mm(s.dqkv[here, :], s.wqkv[cols, :], 1, 1), N.rs3)
 
-    grad_sibling(s.slow, s.dqkv, s.gqk_s, N.gqk)
-    sibling_send(s.gqk_s, s.gqk_r, N.gqk)
+    grad_sibling(s.slow, s.dqkv, s.gqk_s, s.gqk_r, N.gqk)
     plane_scatter_pass(N.rs3)
-    gwi.step1()
     grad_own(s.slow, s.dqkv, s.gqk_r, gqk, N.gqk)
     gwi.step2()
+    gwo.step1()
 
     low_sum = jnp.sum(s.dqkv[...].astype(F32), axis=0, keepdims=True)
     pcols = wide_slice(p * wid, wid, wid)
@@ -1245,24 +1245,11 @@
             lanes = wide_slice((tc * 4 + z_peers[k]) * 128, 128, 128)
             remote(s.smg.at[:, lanes], s.sma.at[cc * 4 + k], N.sma, (N.sma, cc, k), dev(tc, z_peers[k], p))
     sent(s.smg.at[:, pl.ds(0, 7 * 128)], N.sma)
+    gwo.step2()
 
     total = s.first[...] + plane_scatter_sum(N.rs3)
     s.igl[...] = total.astype(BF16)
     send_home(s.igl, s.igr, N.ig)
-
-    for k in (1, 2, 3):
-        arrived(s.gwo_pr.at[k], (N.gwop, k))
-
-    def gwo_total(zz):
-        value = s.gwo_o[wide_slice(zz * zrows + p * rows, rows, rows), :]
-        for k in (1, 2, 3):
-            value = value + s.gwo_pr[k, zz].astype(F32)
-        return value
-
-    for k in (2, 3, 1):
-        s.gwo_zs[z_peers[k]] = gwo_total(z_peers[k]).astype(BF16)
-    s.gwo_t[...] = gwo_total(z)
-    gwo.step0()
 
     gwi.step3()
 
@@ -1276,10 +1263,9 @@
 
     s.gwi_p[...] = s.gwi_o[...].astype(BF16)
     plane_rows(s.gwi_p, s.gwi_pr, N.gwip)
+    gqk.step1()
     gfo.step3()
     dwfo_ref[...] = s.gfo_o[...]
-    gqk.step1()
-    gwo.step1()
 
     def dwin_piece(k):
         if k:
@@ -1304,9 +1290,8 @@
     for k in (1, 2, 3):
         remote(s.smb, s.smb_r.at[k], N.smb, (N.smb, k), dev(c, z, plane_peers[k]))
     sent(s.smb_r.at[pl.ds(0, 3)], N.smb)
-
     gqk.step2()
-    gwo.step2()
+
     arrived(s.outr, N.out)
     out_ref[...] = s.outr[...]
     for k in range(4):

time: 189 us -> 179 us (0.947)
  Pallas kernels: 175 us -> 164 us
    pallas_call x1, Pallas kernels: 175 us -> 164 us  [fused_local(): pl.pallas_call(functools.partial(fused, plan, tok, model, hidden), out_sh...]
where the time goes in v3:
time: 179 us; the launch traced here: 177 us
  Pallas kernels  164 us (92%)
  local copies, waits for them, and re-layouts  10.6 us (6%)
  other arithmetic  2.2 us (1%)
    pallas_call x1, Pallas kernels, fused_local(): pl.pallas_call(functools.partial(fused, plan, tok, model, hidden), out_sh...  164 us
    unnamed x42, local copies, waits for them, and re-layouts  9.39 us

profile of v3, /device:TPU:1, one launch (start us, length us, event | category | flops | bytes accessed | tf_op | source)
XLA Modules:
  0.0 177.4 jit_solution(18036033564383408489)
XLA Ops:
  0.7 0.1 pad.16.clone
  0.8 0.6 copy-done.7
  1.4 0.0 copy-done.5
  1.4 0.7 copy-done.8
  2.2 0.6 copy-done.10
  2.8 0.0 copy-done.13
  2.9 0.6 copy-done.9
  3.5 0.7 fusion.2.refs_3_
  4.2 0.7 select_maximum_fusion.refs_4_
  4.8 0.2 multiply_sine_fusion
  5.0 0.6 pad_maximum_fusion.refs_2_
  5.7 163.8 %shard_map.289 = (bf16[2,64,1024]{2,1,0:T(8,128)(2,1)}, bf16[2,64,1024]{2,1,0:T(8,128)(2,1)}, f32[32,3072]{1,0:T(8,128)}, f32[32,1024]{1,0:T(8,128)}, f32[32,409...) custom-call(bf16[2,64,1024]{2,1,0:T(8,128)(2,1)} %refs_0_.1, bf16[2,64,1024]{2,1,0:T(8,128)(2,1)} %refs_1_.1, ...), custom_call_target="tpu_custom_call" | custom-call | tf_op jit(solution)/shard_map/pallas_call | solution.py:1366
  169.5 0.7 copy-done.6
  170.2 0.5 slice_bitcast_fusion.3
  170.7 0.1 constant_dynamic-slice_fusion
  170.8 0.5 slice_bitcast_fusion
  171.3 1.7 copy.41
  173.1 0.7 copy.42
  173.8 0.7 copy.43
  174.5 0.2 copy-done.4
  174.8 0.7 copy.44
  175.4 0.8 copy.45
  176.2 0.4 copy-done
  176.7 0.8 copy.46
  (33 shorter events, 0.1 us)
Async XLA Ops:
  0.7 0.7 copy-start.7
  0.7 0.7 copy-start.5
  1.4 0.8 copy-start.15
  1.4 0.8 copy-start.16
  1.4 0.8 copy-start.17
  1.4 0.7 copy-start.8
  1.4 0.8 copy-start.14
  2.1 0.7 copy-start.10
  2.1 0.7 copy-start.11
  2.1 0.7 copy-start.12
  2.1 0.7 copy-start.13
  2.8 0.7 copy-start.9
  169.5 0.7 copy-start.6
  171.3 1.7 copy-start.3
  171.3 2.4 %copy-start.2 = (f32[32,3072]{1,0:T(8,128)S(1)}, f32[32,3072]{1,0:T(8,128)}, u32[]{:S(2)}) copy-start(f32[32,3072]{1,0:T(8,128)} %get-tuple-element.58) | copy-start | bytes 1179652
  173.8 1.0 copy-start.4
  173.8 1.7 copy-start.1
  175.4 1.2 copy-start
